TPU v7x, 512 devices: a whole 4x4x16 slice. The times are simulated.
512 devices in a mesh: band: 8 (over x, core), pw: 64 (over z, y).
Axes of the slice: x: 4, y: 4, z: 16, core: 2. Of those that a mesh axis runs over, the one named last changes fastest.
Arguments:
- orbital_coefficients: float32 [8, 2, 128, 128, 128], P('band', None, 'pw'), may hold values from -6 to 6
- sphere_halfwidth: int32 [128, 128], P('pw'), may hold values from -1 to 63, as said below
- occupation: float32 [8], P('band'), may hold values from 0.5 to 2
- local_potential: float32 [256, 256, 256], P(None, 'pw'), may hold values from -6 to 6
- stencil_corner: int32 [64, 64, 128], P('pw'), may hold values from 0 to 262143, as said below
- stencil_weight: float32 [8, 64, 64, 128], P(None, 'pw'), may hold values from -3 to 3
- point_count: int32 [64, 64], P('pw'), may hold values from 0 to 128, as said below
Outputs:
- local_action: float32 [8, 2, 128, 128, 128], P('band', None, 'pw')
- fit_potential: float32 [64, 64, 128], P('pw')
Inputs may be any that keep to these rules, and one draw needn't show every extreme that they name: `sphere_halfwidth`: in every draw the kept columns form one sphere centred at frequency zero that reaches the cube's faces; -1 marks an empty column. `stencil_corner`: each corner is x * 4 + y times 256 plus z, with x and z in 0 to 255 and y in 0 to 3. `point_count`: in every draw some tile has all 128 slots live from every source, and every source has some block with all 128 slots live.
All inputs are finite; a program needn't handle non-finite values.
Results may differ from a plain program's by a relative error of at most 0.0003.
Values sent between devices are 32-bit elements; how exact they have to be, the bound alone decides.
A program may use at most 64 MiB of HBM per device.

v0:
```python
import math

import jax
import jax.numpy as jnp
from jax import lax
from jax.sharding import PartitionSpec as P

hartree_scale = 200.0
exact_mode = lax.Precision.HIGHEST


def shifted(value, axis, steps):
    count = lax.axis_size(axis)
    pairs = [(source, (source + steps) % count) for source in range(count)]
    return lax.ppermute(value, axis, pairs)


def phases(frequency, grid_size):
    position = jnp.arange(grid_size, dtype=jnp.int32)
    product = jnp.remainder(frequency[:, None] * position[None, :], grid_size)
    angle = product.astype(jnp.float32) * (2.0 * math.pi / grid_size)
    return (jnp.cos(angle), jnp.sin(angle))


def inverse_table(frequency, grid_size):
    cosine, sine = phases(frequency, grid_size)
    from_real = jnp.stack([cosine, sine], axis=1)
    from_imag = jnp.stack([-sine, cosine], axis=1)
    return jnp.stack([from_real, from_imag], axis=0)


def forward_table(frequency, grid_size):
    cosine, sine = phases(frequency, grid_size)
    from_real = jnp.stack([cosine.T, -sine.T], axis=1)
    from_imag = jnp.stack([sine.T, cosine.T], axis=1)
    return jnp.stack([from_real, from_imag], axis=0)


def transform(operand, matrix, target_axis, component_axis):
    result = lax.dot_general(
        operand,
        matrix,
        (((component_axis, target_axis), (0, 1)), ((), ())),
        precision=exact_mode,
        preferred_element_type=jnp.float32,
    )
    dimensions = operand.ndim
    return jnp.moveaxis(result, (dimensions - 2, dimensions - 1), (component_axis, target_axis))


def kernel_values(start_x, count_x, start_y, count_y, grid_size):

    def signed(start, count):
        frequency = start + jnp.arange(count, dtype=jnp.int32)
        return jnp.where(frequency < grid_size // 2, frequency, frequency - grid_size)

    along_x = signed(start_x, count_x)
    along_y = signed(start_y, count_y)
    along_z = signed(0, grid_size)
    square = along_x[:, None, None] ** 2 + along_y[None, :, None] ** 2 + along_z[None, None, :] ** 2
    return jnp.where(square > 0, hartree_scale / jnp.maximum(square, 1).astype(jnp.float32), 0.0)


def body(
    orbital_coefficients,
    sphere_halfwidth,
    occupation,
    local_potential,
    stencil_corner,
    stencil_weight,
    point_count,
):
    cube_size = orbital_coefficients.shape[3]
    grid_size = local_potential.shape[0]
    slab_depth = local_potential.shape[1]
    slot_count = stencil_corner.shape[2]
    cube_freq = jnp.arange(cube_size, dtype=jnp.int32) - cube_size // 2
    sphere_mask = (jnp.abs(cube_freq)[None, None, :] <= sphere_halfwidth[:, :, None]).astype(
        jnp.float32
    )
    scale_in = float(cube_size) ** (-1.5)
    scale_out = float(cube_size) ** 1.5 / float(grid_size) ** 3
    inverse_cube = inverse_table(cube_freq, grid_size)
    forward_cube = forward_table(cube_freq, grid_size)
    coefficient = orbital_coefficients * (sphere_mask * scale_in)[None, None]
    partial_section = transform(coefficient, inverse_cube, 4, 1)
    partial_section = transform(partial_section, inverse_cube, 3, 1)
    orbital = transform(
        lax.all_to_all(partial_section, "pw", split_axis=3, concat_axis=2, tiled=True),
        inverse_cube,
        2,
        1,
    )
    partial_density = jnp.sum(
        occupation[:, None, None, None] * (orbital[:, 0] ** 2 + orbital[:, 1] ** 2), axis=0
    )
    product = orbital * local_potential[None, None]
    forward_section = transform(product, forward_cube, 2, 1)
    pencil = lax.all_to_all(forward_section, "pw", split_axis=2, concat_axis=3, tiled=True)
    pencil = transform(pencil, forward_cube, 3, 1)
    spectrum_cube = transform(pencil, forward_cube, 4, 1)
    local_action = spectrum_cube * (sphere_mask * scale_out)[None, None]
    grid_freq = jnp.arange(grid_size, dtype=jnp.int32)
    forward_grid = forward_table(grid_freq, grid_size)
    inverse_grid = inverse_table(grid_freq, grid_size)
    pw_count = lax.axis_size("pw")
    band_count = lax.axis_size("band")
    x_block = grid_size // pw_count
    x_start = lax.axis_index("pw") * x_block
    inverse_norm = 1.0 / float(grid_size) ** 3
    y_block = grid_size // band_count
    y_start = lax.axis_index("band") * y_block
    density_part = lax.psum_scatter(partial_density, "band", scatter_dimension=2, tiled=True)
    spectrum = transform(density_part[None], forward_grid[0:1], 1, 0)
    spectrum = lax.all_to_all(spectrum, "pw", split_axis=1, concat_axis=2, tiled=True)
    spectrum = transform(spectrum, forward_grid, 2, 0)
    spectrum = lax.all_to_all(spectrum, "band", split_axis=2, concat_axis=3, tiled=True)
    spectrum = transform(spectrum, forward_grid, 3, 0)
    spectrum = spectrum * kernel_values(x_start, x_block, y_start, y_block, grid_size)[None]
    spectrum = transform(spectrum, inverse_grid, 3, 0)
    spectrum = lax.all_to_all(spectrum, "band", split_axis=3, concat_axis=2, tiled=True)
    spectrum = transform(spectrum, inverse_grid, 2, 0)
    spectrum = lax.all_to_all(spectrum, "pw", split_axis=2, concat_axis=1, tiled=True)
    hartree_part = transform(spectrum, inverse_grid[:, :, 0:1], 1, 0)[0] * inverse_norm
    hartree = lax.all_gather(hartree_part, "band", axis=2, tiled=True)
    upper_plane = shifted(hartree[:, 0:1, :], "pw", -1)
    extended = jnp.concatenate([hartree, upper_plane], axis=1)
    flattened = extended.reshape(-1)
    plane_cells = slab_depth * grid_size
    request = lax.all_to_all(stencil_corner, "pw", split_axis=1, concat_axis=0, tiled=True)
    coord_x = request // plane_cells
    coord_y = request // grid_size % slab_depth
    coord_z = request % grid_size
    gathered = []
    for corner in range(8):
        step_x = corner // 4
        step_y = corner // 2 % 2
        step_z = corner % 2
        cell_index = (
            (coord_x + step_x) % grid_size * (slab_depth + 1) + coord_y + step_y
        ) * grid_size + (coord_z + step_z) % grid_size
        gathered.append(flattened[cell_index])
    stacked = jnp.stack(gathered, axis=0)
    sampled = lax.all_to_all(stacked, "pw", split_axis=1, concat_axis=2, tiled=True)
    summed = jnp.sum(stencil_weight * sampled, axis=0)
    live_slot = jnp.arange(slot_count, dtype=jnp.int32)[None, None, :] < point_count[:, :, None]
    fit_potential = jnp.where(live_slot, summed, 0.0)
    return (local_action, fit_potential)


def solution(mesh):
    placed = (
        P("band", None, "pw", None, None),
        P("pw", None),
        P("band"),
        P(None, "pw", None),
        P("pw", None, None),
        P(None, "pw", None, None),
        P("pw", None),
    )
    return jax.shard_map(
        body,
        mesh=mesh,
        in_specs=placed,
        out_specs=(P("band", None, "pw", None, None), P("pw", None, None)),
        check_vma=False,
    )
```

profile of v0, /device:TPU:1, one launch (start us, length us, event | category | flops | bytes accessed | tf_op | source)
XLA Modules:
  0.0 734.4 jit_solution(2443056056476492475)
XLA Ops:
  10.3 1.3 copy.52
  11.6 19.3 %all-to-all-start = ((f32[1,2,2,256,256]{4,1,2,0,3:T(2,128)}), f32[1,2,2,256,256]{4,1,2,0,3:T(2,128)S(1)}, u32[]{:S(2)}, u32[]{:S(2)}) async-start(f32[1,2,2,256,256]{4,1,2,0,3:T(2,128)} %copy.52), calls=%async_computation | async-start | bytes 2097152 | tf_op jit(solution)/shard_map/all_to_all | solution.py:89
  31.6 50.7 %all-to-all-done = f32[1,2,2,256,256]{4,1,2,0,3:T(2,128)S(1)} async-done(((f32[1,2,2,256,256]{4,1,2,0,3:T(2,128)}), f32[1,2,2,256,256]{4,1,2,0,3:T(2,128)S(1)}, u32[]{:S(2)}, u32[]{:S(2)}) %all-to-all-start) | async-done | bytes 1048608 | tf_op jit(solution)/shard_map/all_to_all | solution.py:89
  83.2 1.9 convolution_bitcast_fusion
  85.1 1.1 fusion.14
  88.2 31.8 %reduce-scatter.2.cloned.1.call-done = f32[256,4,32]{0,2,1:T(8,128)} async-done(((f32[256,4,256]{0,2,1:T(8,128)}), f32[256,4,32]{0,2,1:T(8,128)}) %reduce-scatter.2.cloned.1.call-update) | async-done | bytes 131088 | tf_op jit(solution)/shard_map/reduce_scatter | solution.py:113
  120.0 2.0 fusion.33
  122.0 1.4 copy.63
  123.5 1.4 reshape.1541
  124.8 14.7 %all-to-all-start.2 = ((f32[64,1,1024]{2,1,0:T(1,128)}), f32[64,1,1024]{2,1,0:T(1,128)}, u32[]{:S(2)}, u32[]{:S(2)}) async-start(f32[64,1,1024]{2,1,0:T(1,128)} %reshape.1541), calls=%async_computation.3 | async-start | bytes 524288 | tf_op jit(solution)/shard_map/all_to_all | solution.py:115
  140.6 1.2 fusion.35
  141.8 1.3 pad_maximum_fusion.1
  143.3 13.6 %all-to-all-done.2 = f32[64,1,1024]{2,1,0:T(1,128)} async-done(((f32[64,1,1024]{2,1,0:T(1,128)}), f32[64,1,1024]{2,1,0:T(1,128)}, u32[]{:S(2)}, u32[]{:S(2)}) %all-to-all-start.2) | async-done | bytes 262176 | tf_op jit(solution)/shard_map/all_to_all | solution.py:115
  157.4 2.2 reduce.1
  159.6 1.5 reshape.1542
  161.2 1.4 copy.64
  163.8 2.0 convolution_bitcast_fusion.8
  165.8 1.3 copy.68
  167.1 3.0 reshape.1543
  170.0 10.1 %all-to-all-start.3 = ((f32[8,1,8192]{2,1,0:T(1,128)}), f32[8,1,8192]{2,1,0:T(1,128)}, u32[]{:S(2)}, u32[]{:S(2)}) async-start(f32[8,1,8192]{2,1,0:T(1,128)} %reshape.1543), calls=%async_computation.4 | async-start | bytes 524288 | tf_op jit(solution)/shard_map/all_to_all | solution.py:117
  180.9 5.8 all-to-all-done.3
  186.8 2.2 reduce.2
  189.0 1.9 reshape.1544
  190.9 2.8 copy.151
  193.7 1.5 all_to_all.105
  195.2 1.9 fusion.9
  197.9 1.3 copy.73
  199.2 2.3 reshape.1545
  201.5 10.6 %all_to_all.126 = f32[8,1,8192]{2,1,0:T(1,128)} all-to-all(f32[8,1,8192]{2,1,0:T(1,128)S(1)} %reshape.1545), channel_id=1, replica_groups=mesh['band'=8,'pw'=64] {'band'}, dimensions={0} | all-to-all | bytes 524288 | tf_op jit(solution)/shard_map/all_to_all | solution.py:121
  212.1 5.7 all-to-all-start.6
  217.8 2.2 reduce.3
  220.0 1.9 reshape.1546
  221.9 2.8 copy.150
  224.7 1.5 reshape.1535
  226.2 1.4 convolution_bitcast_fusion.5
  227.6 1.6 copy.76
  229.3 1.8 reshape.1547
  231.0 14.5 %all-to-all-start.5 = ((f32[64,1,1024]{2,1,0:T(1,128)}), f32[64,1,1024]{2,1,0:T(1,128)S(1)}, u32[]{:S(2)}, u32[]{:S(2)}) async-start(f32[64,1,1024]{2,1,0:T(1,128)} %reshape.1547), calls=%async_computation.6 | async-start | bytes 524288 | tf_op jit(solution)/shard_map/all_to_all | solution.py:123
  245.5 1.6 copy.56
  248.4 2.8 fusion.3
  251.2 2.3 copy.58
  253.5 10.4 %all-to-all-done.5 = f32[64,1,1024]{2,1,0:T(1,128)S(1)} async-done(((f32[64,1,1024]{2,1,0:T(1,128)}), f32[64,1,1024]{2,1,0:T(1,128)S(1)}, u32[]{:S(2)}, u32[]{:S(2)}) %all-to-all-start.5) | async-done | bytes 262176 | tf_op jit(solution)/shard_map/all_to_all | solution.py:123
  263.9 8.4 %all-to-all-start.1 = ((f32[1,2,128,4,256]{4,1,3,0,2:T(2,128)}), f32[1,2,128,4,256]{4,1,3,0,2:T(2,128)}, u32[]{:S(2)}, u32[]{:S(2)}) async-start(f32[1,2,128,4,256]{4,1,3,0,2:T(2,128)} %copy.58), calls=%async_computation.1 | async-start | bytes 2097152 | tf_op jit(solution)/shard_map/all_to_all | solution.py:99
  272.6 1.3 reduce.4
  276.2 2.4 fusion.11
  278.7 32.2 %all-gather.3.cloned.1.call-done = f32[1,256,4,256]{1,3,2,0:T(8,128)} async-done(((f32[1,256,4,32]{1,3,2,0:T(8,128)}), f32[1,256,4,256]{1,3,2,0:T(8,128)}) %all-gather.3.cloned.1.call-update) | async-done | bytes 1048592 | tf_op jit(solution)/shard_map/all_gather | solution.py:125
  311.8 7.9 %collective-permute-start = (f32[256,1,256]{0,2,1:T(8,128)S(1)}, f32[256,1,256]{0,2,1:T(8,128)S(1)}, u32[]{:S(2)}, u32[]{:S(2)}) collective-permute-start(f32[256,1,256]{0,2,1:T(8,128)S(1)} %slice.36), channel_id=1, source_target_pairs={{0,63},{1,0},{2,1},{3,2},{4,3},{5,4},{6,5},{7,6},{8,7},{9,8},{10,9... | collective-permute-start | bytes 786440 | tf_op jit(solution)/shard_map/ppermute | solution.py:15
  319.7 1.5 fusion.96
  321.2 1.5 fusion.94
  322.7 2.6 collective-permute-done
  325.3 1.3 pad_maximum_fusion
  326.6 1.1 copy.80
  328.0 45.7 %gather_fusion.7 = f32[8192]{0:T(1024)S(1)} fusion(f32[327680]{0:T(1024)S(1)} %reshape.1420, s32[8192]{0:T(1024)} %get-tuple-element.8), kind=kCustom, calls=%fused_computation.7 | custom fusion | bytes 98304 | tf_op jit(solution)/shard_map/gather | solution.py:142
  373.7 45.5 %gather_fusion.6 = f32[8192]{0:T(1024)S(1)} fusion(f32[327680]{0:T(1024)S(1)} %reshape.1420, s32[8192]{0:T(1024)S(1)} %copy-done.18), kind=kCustom, calls=%fused_computation.6 | custom fusion | bytes 98304 | tf_op jit(solution)/shard_map/gather | solution.py:142
  419.2 45.5 %gather_fusion.5 = f32[8192]{0:T(1024)S(1)} fusion(f32[327680]{0:T(1024)S(1)} %reshape.1420, s32[8192]{0:T(1024)S(1)} %copy-done.17), kind=kCustom, calls=%fused_computation.5 | custom fusion | bytes 98304 | tf_op jit(solution)/shard_map/gather | solution.py:142
  464.8 45.5 %gather_fusion.4 = f32[8192]{0:T(1024)S(1)} fusion(f32[327680]{0:T(1024)S(1)} %reshape.1420, s32[8192]{0:T(1024)S(1)} %copy-done.16), kind=kCustom, calls=%fused_computation.4 | custom fusion | bytes 98304 | tf_op jit(solution)/shard_map/gather | solution.py:142
  510.4 45.5 %gather_fusion.3 = f32[8192]{0:T(1024)S(1)} fusion(f32[327680]{0:T(1024)S(1)} %reshape.1420, s32[8192]{0:T(1024)S(1)} %copy-done.12), kind=kCustom, calls=%fused_computation.3 | custom fusion | bytes 98304 | tf_op jit(solution)/shard_map/gather | solution.py:142
  555.9 45.5 %gather_fusion.2 = f32[8192]{0:T(1024)S(1)} fusion(f32[327680]{0:T(1024)S(1)} %reshape.1420, s32[8192]{0:T(1024)S(1)} %copy-done.15), kind=kCustom, calls=%fused_computation.2 | custom fusion | bytes 98304 | tf_op jit(solution)/shard_map/gather | solution.py:142
  601.5 45.5 %gather_fusion.1 = f32[8192]{0:T(1024)S(1)} fusion(f32[327680]{0:T(1024)S(1)} %reshape.1420, s32[8192]{0:T(1024)S(1)} %copy-done.14), kind=kCustom, calls=%fused_computation.1 | custom fusion | bytes 98304 | tf_op jit(solution)/shard_map/gather | solution.py:142
  647.0 45.5 %gather_fusion = f32[8192]{0:T(1024)S(1)} fusion(f32[327680]{0:T(1024)S(1)} %reshape.1420, s32[8192]{0:T(1024)S(1)} %copy-done.13), kind=kCustom, calls=%fused_computation | custom fusion | bytes 98304 | tf_op jit(solution)/shard_map/gather | solution.py:142
  693.7 13.6 %all-to-all-start.7 = ((f32[8,64,1,128]{3,0,2,1:T(8,128)}), f32[8,64,1,128]{3,0,2,1:T(8,128)S(1)}, u32[]{:S(2)}, u32[]{:S(2)}) async-start(f32[8,64,1,128]{3,0,2,1:T(8,128)} %stack.131), calls=%async_computation.8 | async-start | bytes 524288 | tf_op jit(solution)/shard_map/all_to_all | solution.py:144
  707.2 1.5 copy.59
  709.8 1.8 convolution_bitcast_fusion.2
  713.3 12.8 %all-to-all-done.7 = f32[8,64,1,128]{3,0,2,1:T(8,128)S(1)} async-done(((f32[8,64,1,128]{3,0,2,1:T(8,128)}), f32[8,64,1,128]{3,0,2,1:T(8,128)S(1)}, u32[]{:S(2)}, u32[]{:S(2)}) %all-to-all-start.7) | async-done | bytes 262176 | tf_op jit(solution)/shard_map/all_to_all | solution.py:144
  (79 shorter events, 20.1 us)
Async XLA Ops:
  7.2 1.5 copy-start.11
  11.6 70.7 %all-to-all-start = ((f32[1,2,2,256,256]{4,1,2,0,3:T(2,128)}), f32[1,2,2,256,256]{4,1,2,0,3:T(2,128)S(1)}, u32[]{:S(2)}, u32[]{:S(2)}) async-start(f32[1,2,2,256,256]{4,1,2,0,3:T(2,128)} %copy.52), calls=%async_computation | async-start | bytes 2097152 | tf_op jit(solution)/shard_map/all_to_all | solution.py:89
  30.9 89.0 %reduce-scatter.2.cloned.1.call-start = ((), (), s32[]{:S(2)}) async-start(), calls=%async_computation.9 | async-start | bytes 1179648 | tf_op jit(solution)/shard_map/reduce_scatter | solution.py:113
  88.2 31.8 %copy-start.9 = (f32[256,1,256]{2,0,1:T(8,128)}, f32[256,1,256]{2,0,1:T(8,128)S(1)}, u32[]{:S(2)}) copy-start(f32[256,1,256]{2,0,1:T(8,128)S(1)} %fusion.57) | copy-start | bytes 786436
  124.8 32.1 %all-to-all-start.2 = ((f32[64,1,1024]{2,1,0:T(1,128)}), f32[64,1,1024]{2,1,0:T(1,128)}, u32[]{:S(2)}, u32[]{:S(2)}) async-start(f32[64,1,1024]{2,1,0:T(1,128)} %reshape.1541), calls=%async_computation.3 | async-start | bytes 524288 | tf_op jit(solution)/shard_map/all_to_all | solution.py:115
  141.8 1.3 copy-start.1
  141.8 1.4 copy-start.3
  162.6 1.2 copy-start
  170.0 16.7 %all-to-all-start.3 = ((f32[8,1,8192]{2,1,0:T(1,128)}), f32[8,1,8192]{2,1,0:T(1,128)}, u32[]{:S(2)}, u32[]{:S(2)}) async-start(f32[8,1,8192]{2,1,0:T(1,128)} %reshape.1543), calls=%async_computation.4 | async-start | bytes 524288 | tf_op jit(solution)/shard_map/all_to_all | solution.py:117
  212.1 19.0 %all-to-all-start.6 = ((s32[1,64,128]{2,0,1:T(1,128)}), s32[1,64,128]{2,0,1:T(1,128)}, u32[]{:S(2)}, u32[]{:S(2)}) async-start(s32[1,64,128]{2,0,1:T(1,128)} %bitcast.297), calls=%async_computation.7 | async-start | bytes 65536 | tf_op jit(solution)/shard_map/all_to_all | solution.py:130
  231.0 32.9 %all-to-all-start.5 = ((f32[64,1,1024]{2,1,0:T(1,128)}), f32[64,1,1024]{2,1,0:T(1,128)S(1)}, u32[]{:S(2)}, u32[]{:S(2)}) async-start(f32[64,1,1024]{2,1,0:T(1,128)} %reshape.1547), calls=%async_computation.6 | async-start | bytes 524288 | tf_op jit(solution)/shard_map/all_to_all | solution.py:123
  247.6 0.7 copy-start.5
  247.7 0.8 copy-start.7
  263.9 429.8 %all-to-all-start.1 = ((f32[1,2,128,4,256]{4,1,3,0,2:T(2,128)}), f32[1,2,128,4,256]{4,1,3,0,2:T(2,128)}, u32[]{:S(2)}, u32[]{:S(2)}) async-start(f32[1,2,128,4,256]{4,1,3,0,2:T(2,128)} %copy.58), calls=%async_computation.1 | async-start | bytes 2097152 | tf_op jit(solution)/shard_map/all_to_all | solution.py:99
  272.3 38.5 %all-gather.3.cloned.1.call-start = ((), (), s32[]{:S(2)}) async-start(), calls=%async_computation.10 | async-start | bytes 1179648 | tf_op jit(solution)/shard_map/all_gather | solution.py:125
  275.0 1.0 copy-start.2
  275.0 1.2 copy-start.4
  311.8 13.5 %collective-permute-start = (f32[256,1,256]{0,2,1:T(8,128)S(1)}, f32[256,1,256]{0,2,1:T(8,128)S(1)}, u32[]{:S(2)}, u32[]{:S(2)}) collective-permute-start(f32[256,1,256]{0,2,1:T(8,128)S(1)} %slice.36), channel_id=1, source_target_pairs={{0,63},{1,0},{2,1},{3,2},{4,3},{5,4},{6,5},{7,6},{8,7},{9,8},{10,9... | collective-permute-start | bytes 786440 | tf_op jit(solution)/shard_map/ppermute | solution.py:15
  328.0 45.7 %copy-start.18 = (s32[8192]{0:T(1024)S(1)}, s32[8192]{0:T(1024)}, u32[]{:S(2)}) copy-start(s32[8192]{0:T(1024)} %get-tuple-element.22) | copy-start | bytes 98308
  373.7 45.6 %copy-start.17 = (s32[8192]{0:T(1024)S(1)}, s32[8192]{0:T(1024)}, u32[]{:S(2)}) copy-start(s32[8192]{0:T(1024)} %get-tuple-element.23) | copy-start | bytes 98308
  419.2 45.6 %copy-start.16 = (s32[8192]{0:T(1024)S(1)}, s32[8192]{0:T(1024)}, u32[]{:S(2)}) copy-start(s32[8192]{0:T(1024)} %get-tuple-element.24) | copy-start | bytes 98308
  464.8 45.6 %copy-start.12 = (s32[8192]{0:T(1024)S(1)}, s32[8192]{0:T(1024)}, u32[]{:S(2)}) copy-start(s32[8192]{0:T(1024)} %get-tuple-element.31) | copy-start | bytes 98308
  510.4 45.6 %copy-start.15 = (s32[8192]{0:T(1024)S(1)}, s32[8192]{0:T(1024)}, u32[]{:S(2)}) copy-start(s32[8192]{0:T(1024)} %get-tuple-element.30) | copy-start | bytes 98308
  555.9 45.6 %copy-start.14 = (s32[8192]{0:T(1024)S(1)}, s32[8192]{0:T(1024)}, u32[]{:S(2)}) copy-start(s32[8192]{0:T(1024)} %get-tuple-element.29) | copy-start | bytes 98308
  601.5 45.6 %copy-start.13 = (s32[8192]{0:T(1024)S(1)}, s32[8192]{0:T(1024)}, u32[]{:S(2)}) copy-start(s32[8192]{0:T(1024)} %get-tuple-element.28) | copy-start | bytes 98308
  693.7 32.5 %all-to-all-start.7 = ((f32[8,64,1,128]{3,0,2,1:T(8,128)}), f32[8,64,1,128]{3,0,2,1:T(8,128)S(1)}, u32[]{:S(2)}, u32[]{:S(2)}) async-start(f32[8,64,1,128]{3,0,2,1:T(8,128)} %stack.131), calls=%async_computation.8 | async-start | bytes 524288 | tf_op jit(solution)/shard_map/all_to_all | solution.py:144
  708.7 1.0 copy-start.6
  708.7 1.0 copy-start.8
  711.6 14.6 %copy-start.10 = (f32[8,1,64,128]{3,2,1,0:T(8,128)S(1)}, f32[8,1,64,128]{3,2,1,0:T(8,128)}, u32[]{:S(2)}) copy-start(f32[8,1,64,128]{3,2,1,0:T(8,128)} %param.12) | copy-start | bytes 786436
  711.6 14.8 %copy-start.19 = (s32[1,64]{1,0:T(1,128)S(1)}, s32[1,64]{1,0:T(1,128)}, u32[]{:S(2)}) copy-start(s32[1,64]{1,0:T(1,128)} %param.13) | copy-start | bytes 772
Sparse Core Ops, SparseCore 0:
  86.4 33.5 reduce-scatter.1
  278.8 32.0 all-gather.2
where the time goes:
time: 746 us; the launch traced here: 734 us
  local copies, waits for them, and re-layouts  411 us (55%)
  waiting for transfers between devices  160 us (21%)
  starting transfers between devices  94.4 us (13%)
  other arithmetic  22.6 us (3%)
  matrix products  19.7 us (3%)
  between operations  15.8 us (2%)
  blocking collectives  10.6 us (1%)
    gather x8, local copies, waits for them, and re-layouts, body(): gathered.append(flattened[cell_index])  364 us
    all_to_all x1, waiting for transfers between devices, body(): lax.all_to_all(partial_section, 'pw', split_axis=3, concat_axis=2, tiled=...  50.7 us
    all_gather x1, waiting for transfers between devices, body(): hartree = lax.all_gather(hartree_part, 'band', axis=2, tiled=True)  32.2 us
    reduce_scatter x1, waiting for transfers between devices, body(): lax.psum_scatter(partial_density, 'band', scatter_dimension=2, tiled=True)  31.8 us
    dot_general x12, matrix products, transform(): lax.dot_general(operand, matrix, (((component_axis, target_axis), (0, 1))...  19.7 us
    all_to_all x1, starting transfers between devices, body(): lax.all_to_all(partial_section, 'pw', split_axis=3, concat_axis=2, tiled=...  19.3 us
    unnamed x50, local copies, waits for them, and re-layouts  19.3 us
  transfers between devices with their start and end apart: 10, of which 8 were waited for; matrix products, arithmetic and copies ran while one was open for 56% of the time, Pallas kernels for 0%

commit v1 on v0

v1 whole, which is shorter than its diff:
```python
import math

import jax
import jax.numpy as jnp
import numpy as np
from jax import lax
from jax.sharding import PartitionSpec as P

HARTREE_SCALE = 200.0
HIGH = lax.Precision.HIGH


def wave_table(positions, modes, grid):
    angle = (np.outer(positions, modes) % grid) * (2.0 * math.pi / grid)
    cosine, sine = np.cos(angle), np.sin(angle)
    return np.stack([np.stack([cosine, -sine], 1), np.stack([sine, cosine], 1)], 0)


def real_basis(grid):
    half = grid // 2
    position = np.arange(grid)
    angle = lambda n: (np.outer(n, position) % grid) * (2.0 * math.pi / grid)
    rows = np.concatenate([np.cos(angle(np.arange(half + 1))), np.sin(angle(np.arange(1, half)))])
    return rows / np.sqrt(np.sum(rows * rows, axis=1, keepdims=True))


def dot(spec, *operands):
    return jnp.einsum(spec, *operands, precision=HIGH, preferred_element_type=jnp.float32)


def body(coefficients, halfwidth, occupation, potential, corner, weight, count):
    wg = coefficients.shape[3]
    ng = potential.shape[0]
    slab = potential.shape[1]
    slots = corner.shape[2]
    bands = lax.axis_size("band")
    tiles = lax.axis_size("pw")
    b = lax.axis_index("band")
    p = lax.axis_index("pw")
    f32 = lambda a: jnp.asarray(a, jnp.float32)
    modes = np.arange(wg) - wg // 2
    wave = wave_table(np.arange(ng), modes, ng)
    scale_in = float(wg) ** -1.5
    scale_out = float(wg) ** 1.5 / float(ng) ** 3
    cube = f32(wave)
    wave_y = f32(wave.reshape(2, tiles, slab, 2, wg))
    mask = (jnp.abs(f32(modes))[None, None, :] <= halfwidth[:, :, None]).astype(jnp.float32)

    share = slots // bands
    packed = jnp.concatenate([weight[:, 0], corner[0].astype(jnp.float32)[None]], 0)
    packed = lax.dynamic_slice_in_dim(packed, b * share, share, 2)
    packed = packed.transpose(1, 0, 2).reshape(tiles, 9 * share)
    packed = lax.all_to_all(packed, "pw", 0, 0, tiled=True)

    masked = coefficients[0] * (mask * scale_in)[None]
    section = dot("edjcm,cimz->deijz", wave_y, masked)
    section = lax.all_to_all(section, "pw", 0, 0, tiled=True)
    cube_x = cube.reshape(2, ng, 2, tiles, wg // tiles)
    section = dot("excpi,pcijz->exjz", cube_x, section)
    orbital = dot("fzcm,cxjm->fxjz", cube, section)
    density = occupation[0] * (orbital[0] ** 2 + orbital[1] ** 2)

    basis_np = real_basis(ng)
    basis = f32(basis_np)
    first = jnp.arange(ng) == 0
    mean = jnp.mean(density, axis=(0, 2))
    spectrum = dot("xjz,lz->xjl", density - mean[None, :, None], basis)
    spectrum = dot("kx,xjl->kjl", basis, spectrum)
    spectrum = spectrum + jnp.where(first[:, None, None] & first[None, None, :], float(ng) * mean[None, :, None], 0.0)
    spectrum = lax.psum_scatter(spectrum, "band", scatter_dimension=0, tiled=True)
    per = ng // bands
    halves = tiles // per
    lanes = ng // halves
    spectrum = spectrum.reshape(per, slab, halves, lanes).transpose(0, 2, 1, 3).reshape(tiles, slab, lanes)
    spectrum = lax.all_to_all(spectrum, "pw", 0, 0, tiled=True).reshape(ng, lanes)
    mean = jnp.mean(spectrum, axis=0)
    spectrum = dot("ky,yl->kl", basis, spectrum - mean[None])
    spectrum = spectrum + jnp.where(first[:, None], math.sqrt(ng) * mean[None], 0.0)
    number = jnp.arange(ng, dtype=jnp.int32)
    number = jnp.where(number <= ng // 2, number, number - ng // 2)
    take = lambda start, size: lax.dynamic_slice_in_dim(number, start, size)
    square = (
        number[:, None] ** 2
        + take((p % halves) * lanes, lanes)[None, :] ** 2
        + take(b * per + p // halves, 1)[:, None] ** 2
    )
    kernel = jnp.where(square > 0, HARTREE_SCALE / jnp.maximum(square, 1).astype(jnp.float32), 0.0)
    planes = (np.arange(tiles)[:, None] * slab + np.arange(slab + 1)[None, :]) % ng
    back = f32(basis_np.T[planes])
    spectrum = dot("tjk,kl->tjl", back, spectrum * kernel)
    spectrum = lax.all_to_all(spectrum, "pw", 0, 0, tiled=True)
    spectrum = lax.all_gather(spectrum, "band", axis=0, tiled=True)
    spectrum = spectrum.reshape(ng, halves, slab + 1, lanes)
    basis_z = basis.reshape(halves, lanes, ng)
    hartree = dot("khjl,hlz->kjz", spectrum, basis_z)
    hartree = dot("kx,kjz->zjx", basis, hartree)

    product = orbital * potential[None]
    product = dot("fzcm,fxjz->cxjm", cube, product)
    product = dot("excpi,exjz->pcijz", cube_x, product)
    product = lax.all_to_all(product, "pw", 0, 0, tiled=True)
    action = dot("edjcm,deijz->cimz", wave_y, product)
    action = action * (mask * scale_out)[None]

    packed = packed.reshape(tiles, 9, share).transpose(1, 0, 2).reshape(9, tiles * share)
    place = packed[8].astype(jnp.int32)
    px, py, pz = place // (slab * ng), place // ng % slab, place % ng
    index_x = jnp.arange(ng, dtype=jnp.int32)
    index_y = jnp.arange(slab + 1, dtype=jnp.int32)
    total = 0.0
    for dz in range(2):
        column = 0.0
        for dx in range(2):
            at_x = index_x[:, None] == ((px + dx) % ng)[None, :]
            for dy in range(2):
                at_y = index_y[:, None] == (py + dy)[None, :]
                w = packed[4 * dx + 2 * dy + dz]
                column = column + jnp.where(at_y[:, None] & at_x[None], w[None, None], 0.0)
        lines = dot("zjx,jxs->zs", hartree, column)
        at_z = index_x[:, None] == ((pz + dz) % ng)[None, :]
        total = total + jnp.sum(jnp.where(at_z, lines, 0.0), axis=0)
    total = lax.all_to_all(total.reshape(tiles, share), "pw", 0, 0, tiled=True)
    total = lax.all_gather(total, "band", axis=1, tiled=True)
    live = jnp.arange(slots, dtype=jnp.int32)[None, :] < count[0][:, None]
    return action[None], jnp.where(live, total, 0.0)[None]


def solution(mesh):
    placed = (
        P("band", None, "pw", None, None),
        P("pw", None),
        P("band"),
        P(None, "pw", None),
        P("pw", None, None),
        P(None, "pw", None, None),
        P("pw", None),
    )
    return jax.shard_map(
        body,
        mesh=mesh,
        in_specs=placed,
        out_specs=(P("band", None, "pw", None, None), P("pw", None, None)),
        check_vma=False,
    )
```

time: 746 us -> 293 us (0.39); the launches traced: 734 us -> 291 us
  local copies, waits for them, and re-layouts: 411 us -> 34.7 us
  waiting for transfers between devices: 160 us -> 110 us
  starting transfers between devices: 94.4 us -> 54.9 us
  blocking collectives: 10.6 us -> 46.6 us
  other arithmetic: 22.6 us -> 6.09 us
    gather x8 -> x0, local copies, waits for them, and re-layouts: 364 us -> none  [body(): gathered.append(flattened[cell_index])]
    all_gather x1, waiting for transfers between devices: 32.2 us -> 0.02 us  [body(): spectrum = lax.all_gather(spectrum, 'band', axis=0, tiled=True)]
    all_to_all x7 -> x5, starting transfers between devices: 86.2 us -> 54.8 us  [the longest x1 19.3 us: body(): section = lax.all_to_all(section, 'pw', 0, 0, tiled=True)]
    all_gather x0 -> x1, blocking collectives: none -> 25 us  [body(): total = lax.all_gather(total, 'band', axis=1, tiled=True)]
    all_to_all x7 -> x5, waiting for transfers between devices: 93.5 us -> 77.1 us  [the longest x1 29.2 us: body(): section = lax.all_to_all(section, 'pw', 0, 0, tiled=True)]
    unnamed x50 -> x45, local copies, waits for them, and re-layouts: 19.3 us -> 3.34 us
    all_to_all x13 -> x4, local copies, waits for them, and re-layouts: 15 us -> 3.05 us  [the longest x2 2.3 us: body(): packed = lax.all_to_all(packed, 'pw', 0, 0, tiled=True)]
    all_to_all x1, blocking collectives: 10.6 us -> 21.5 us  [body(): spectrum = lax.all_to_all(spectrum, 'pw', 0, 0, tiled=True)]
  transfers between devices with their start and end apart: 10 -> 7, of which waited for: 8 -> 6; matrix products, arithmetic and copies ran while one was open for 56% -> 17% of each run, Pallas kernels for 0% -> 0%
where the time goes in v1:
time: 293 us; the launch traced here: 291 us
  waiting for transfers between devices  110 us (38%)
  starting transfers between devices  54.9 us (19%)
  blocking collectives  46.6 us (16%)
  local copies, waits for them, and re-layouts  34.7 us (12%)
  matrix products  22.2 us (8%)
  between operations  16.5 us (6%)
  other arithmetic  6.09 us (2%)
    reduce_scatter x1, waiting for transfers between devices, body(): lax.psum_scatter(spectrum, 'band', scatter_dimension=0, tiled=True)  32.7 us
    all_to_all x1, waiting for transfers between devices, body(): section = lax.all_to_all(section, 'pw', 0, 0, tiled=True)  29.2 us
    all_gather x1, blocking collectives, body(): total = lax.all_gather(total, 'band', axis=1, tiled=True)  25 us
    dot_general x14, matrix products, dot(): jnp.einsum(spec, *operands, precision=HIGH, preferred_element_type=jnp.fl...  22.2 us
    all_to_all x1, blocking collectives, body(): spectrum = lax.all_to_all(spectrum, 'pw', 0, 0, tiled=True)  21.5 us
    all_to_all x1, starting transfers between devices, body(): section = lax.all_to_all(section, 'pw', 0, 0, tiled=True)  19.3 us
    all_to_all x1, starting transfers between devices, body(): lax.all_to_all(spectrum, 'pw', 0, 0, tiled=True).reshape(ng, lanes)  14.4 us
    all_to_all x1, waiting for transfers between devices, body(): lax.all_to_all(spectrum, 'pw', 0, 0, tiled=True).reshape(ng, lanes)  12.9 us
  transfers between devices with their start and end apart: 7, of which 6 were waited for; matrix products, arithmetic and copies ran while one was open for 17% of the time, Pallas kernels for 0%

profile of v1, /device:TPU:1, one launch (start us, length us, event | category | flops | bytes accessed | tf_op | source)
XLA Modules:
  0.0 290.8 jit_solution(741918760410658620)
XLA Ops:
  7.2 0.7 convert_element_type.37
  7.9 0.7 compare_select_fusion
  8.8 1.5 convolution_bitcast_fusion.5
  10.3 1.2 copy.62
  11.5 19.3 %all-to-all-start = ((f32[64,2,2,4,128]{4,3,2,1,0:T(4,128)}), f32[64,2,2,4,128]{4,3,2,1,0:T(4,128)S(1)}, u32[]{:S(2)}, u32[]{:S(2)}) async-start(f32[64,2,2,4,128]{4,3,2,1,0:T(4,128)} %copy.62), calls=%async_computation | async-start | bytes 1048576 | tf_op jit(solution)/shard_map/all_to_all | solution.py:57
  31.6 29.2 %all-to-all-done = f32[64,2,2,4,128]{4,3,2,1,0:T(4,128)S(1)} async-done(((f32[64,2,2,4,128]{4,3,2,1,0:T(4,128)}), f32[64,2,2,4,128]{4,3,2,1,0:T(4,128)S(1)}, u32[]{:S(2)}, u32[]{:S(2)}) %all-to-all-start) | async-done | bytes 524320 | tf_op jit(solution)/shard_map/all_to_all | solution.py:57
  60.8 0.8 convolution_bitcast_fusion.3
  61.6 1.0 convolution_bitcast_fusion
  62.6 0.3 fusion.67
  62.9 0.7 fusion.59
  63.6 1.6 convolution_add_fusion
  65.3 32.7 %reduce-scatter.2.cloned.1.call-done = f32[32,4,256]{2,0,1:T(8,128)} async-done(((f32[256,4,256]{2,0,1:T(8,128)}), f32[32,4,256]{2,0,1:T(8,128)}) %reduce-scatter.2.cloned.1.call-update) | async-done | bytes 131088 | tf_op jit(solution)/shard_map/reduce_scatter | solution.py:70
  97.9 0.9 fusion.83
  98.9 0.7 copy.74
  99.6 14.4 %all-to-all-start.3 = ((f32[64,4,128]{2,1,0:T(4,128)}), f32[64,4,128]{2,1,0:T(4,128)S(1)}, u32[]{:S(2)}, u32[]{:S(2)}) async-start(f32[64,4,128]{2,1,0:T(4,128)} %bitcast.43), calls=%async_computation.4 | async-start | bytes 262144 | tf_op jit(solution)/shard_map/all_to_all | solution.py:75
  114.1 0.6 dynamic_slice.11
  116.0 12.9 %all-to-all-done.3 = f32[64,4,128]{2,1,0:T(4,128)S(1)} async-done(((f32[64,4,128]{2,1,0:T(4,128)}), f32[64,4,128]{2,1,0:T(4,128)S(1)}, u32[]{:S(2)}, u32[]{:S(2)}) %all-to-all-start.3) | async-done | bytes 131104 | tf_op jit(solution)/shard_map/all_to_all | solution.py:75
  129.1 0.3 fusion.56
  129.4 0.3 fusion.85
  129.8 21.5 %all_to_all.38 = f32[64,5,128]{2,1,0:T(8,128)S(1)} all-to-all(f32[64,5,128]{2,1,0:T(8,128)S(1)} %copy.75), channel_id=1, replica_groups=mesh['band'=8,'pw'=64] {'pw'}, dimensions={0} | all-to-all | bytes 327680 | tf_op jit(solution)/shard_map/all_to_all | solution.py:91
  151.3 0.7 copy.76
  152.4 0.7 copy.71
  153.1 6.0 %all-to-all-start.2 = ((f32[64,1,144]{2,1,0:T(1,128)}), f32[64,1,144]{2,1,0:T(1,128)}, u32[]{:S(2)}, u32[]{:S(2)}) async-start(f32[64,1,144]{2,1,0:T(1,128)} %copy.71), calls=%async_computation.2 | async-start | bytes 131072 | tf_op jit(solution)/shard_map/all_to_all | solution.py:53
  159.1 1.4 copy.64
  160.5 12.2 %all-to-all-done.2 = f32[64,1,144]{2,1,0:T(1,128)} async-done(((f32[64,1,144]{2,1,0:T(1,128)}), f32[64,1,144]{2,1,0:T(1,128)}, u32[]{:S(2)}, u32[]{:S(2)}) %all-to-all-start.2) | async-done | bytes 36896 | tf_op jit(solution)/shard_map/all_to_all | solution.py:53
  172.7 1.6 copy.72
  174.3 1.5 fusion.84
  175.8 1.4 copy.82
  177.2 1.4 broadcast_in_dim.202
  178.6 1.4 copy.81
  180.0 1.4 broadcast_in_dim.200
  181.4 1.4 copy.80
  182.8 1.4 broadcast_in_dim.198
  184.3 1.4 copy.79
  185.6 1.4 broadcast_in_dim.195
  187.1 1.4 copy.73
  188.5 1.4 convert_element_type.40
  189.9 1.4 copy.86
  191.3 1.4 broadcast_in_dim.211
  192.7 1.4 copy.85
  194.1 1.4 broadcast_in_dim.209
  195.5 0.7 copy.84
  196.2 0.8 broadcast_in_dim.207
  197.0 0.7 copy.83
  197.7 0.8 broadcast_in_dim.205
  198.6 1.3 add_select_fusion
  199.9 1.1 iota_compare_fusion.1
  201.0 2.1 fusion.31
  203.1 0.6 convolution_bitcast_fusion.4
  203.7 1.1 copy.67
  204.9 4.6 %all-to-all-start.1 = ((f32[64,2,2,4,128]{4,3,1,2,0:T(4,128)}), f32[64,2,2,4,128]{4,3,1,2,0:T(4,128)S(1)}, u32[]{:S(2)}, u32[]{:S(2)}) async-start(f32[64,2,2,4,128]{4,3,1,2,0:T(4,128)} %copy.67), calls=%async_computation.1 | async-start | bytes 1048576 | tf_op jit(solution)/shard_map/all_to_all | solution.py:101
  209.6 2.0 convolution_bitcast_fusion.2
  211.7 0.7 convolution_bitcast_fusion.1
  212.4 0.2 copy-done.6
  212.7 4.9 %fusion.50 = f32[1024]{0:T(1024)S(1)} fusion(f32[256,5,256]{2,0,1:T(8,128)S(1)} %convolution_bitcast_fusion.1, f32[1024]{0:T(1024)S(1)} %copy-done.11, f32[1024]{0:T(1024)S(1)} %copy-done.12, f32[1024]{0:T(1024)S(1)} %copy-done.13, f32[1024]{0:T(1024)S(1)} %copy-done.14, pred[256,1024]{1,0:T(8,128)(4,1)S(1)} %copy-done.6, ...), kind=kOutput, calls=%fused_computation.51 | convolution fusion | flops 2028469248 | bytes 1869824 | tf_op jit(solution)/shard_map/zjx,jxs->zs/dot_general | solution.py:28
  217.7 4.9 %fusion.47 = f32[1024]{0:T(1024)S(1)} fusion(f32[256,5,256]{2,0,1:T(8,128)S(1)} %convolution_bitcast_fusion.1, f32[1024]{0:T(1024)S(1)} %copy-done.15, f32[1024]{0:T(1024)S(1)} %copy-done.16, f32[1024]{0:T(1024)S(1)} %broadcast_in_dim.207, f32[1024]{0:T(1024)S(1)} %broadcast_in_dim.205, pred[256,1024]{1,0:T(8,128)(4,1)S(1)} %copy-done.6, ...), kind=kOutput, calls=%fused_computation.50 | convolution fusion | flops 2028469248 | bytes 1869824 | tf_op jit(solution)/shard_map/zjx,jxs->zs/dot_general | solution.py:28
  222.7 0.7 add.220
  223.4 10.9 %all-to-all-done.1 = f32[64,2,2,4,128]{4,3,1,2,0:T(4,128)S(1)} async-done(((f32[64,2,2,4,128]{4,3,1,2,0:T(4,128)}), f32[64,2,2,4,128]{4,3,1,2,0:T(4,128)S(1)}, u32[]{:S(2)}, u32[]{:S(2)}) %all-to-all-start.1) | async-done | bytes 524320 | tf_op jit(solution)/shard_map/all_to_all | solution.py:101
  234.2 10.5 %all-to-all-start.5 = ((f32[64,1,16]{2,1,0:T(1,128)}), f32[64,1,16]{2,1,0:T(1,128)S(1)}, u32[]{:S(2)}, u32[]{:S(2)}) async-start(f32[64,1,16]{2,1,0:T(1,128)} %bitcast.54), calls=%async_computation.6 | async-start | bytes 65536 | tf_op jit(solution)/shard_map/all_to_all | solution.py:122
  244.8 0.7 fusion.54
  245.4 0.8 copy.89
  246.3 11.8 %all-to-all-done.5 = f32[64,1,16]{2,1,0:T(1,128)S(1)} async-done(((f32[64,1,16]{2,1,0:T(1,128)}), f32[64,1,16]{2,1,0:T(1,128)S(1)}, u32[]{:S(2)}, u32[]{:S(2)}) %all-to-all-start.5) | async-done | bytes 4128 | tf_op jit(solution)/shard_map/all_to_all | solution.py:122
  258.2 25.0 %all-gather = f32[64,1,128]{0,1,2:T(1,128)S(1)} all-gather(f32[64,1,16]{0,1,2:T(1,128)S(1)} %copy.88), channel_id=2, replica_groups=mesh['band'=8,'pw'=64] {'band'}, dimensions={2}, use_global_device_ids=true | all-gather | bytes 36864 | tf_op jit(solution)/shard_map/all_gather | solution.py:123
  283.3 0.7 copy.90
  (64 shorter events, 1.2 us)
Async XLA Ops:
  7.2 53.6 %copy-start.4 = (f32[2,256,2,64,2,1]{1,3,4,2,0,5:T(8,128)S(1)}, f32[2,256,2,64,2,1]{1,3,4,2,0,5:T(8,128)}, u32[]{:S(2)}) copy-start(f32[2,256,2,64,2,1]{1,3,4,2,0,5:T(8,128)} %constant.166) | copy-start | bytes 1572868
  10.3 51.3 %copy-start.1 = (f32[2,256,2,128,1]{3,1,2,0,4:T(8,128)S(1)}, f32[2,256,2,128,1]{3,1,2,0,4:T(8,128)}, u32[]{:S(2)}) copy-start(f32[2,256,2,128,1]{3,1,2,0,4:T(8,128)} %constant.168) | copy-start | bytes 1572868
  11.5 49.3 %all-to-all-start = ((f32[64,2,2,4,128]{4,3,2,1,0:T(4,128)}), f32[64,2,2,4,128]{4,3,2,1,0:T(4,128)S(1)}, u32[]{:S(2)}, u32[]{:S(2)}) async-start(f32[64,2,2,4,128]{4,3,2,1,0:T(4,128)} %copy.62), calls=%async_computation | async-start | bytes 1048576 | tf_op jit(solution)/shard_map/all_to_all | solution.py:57
  30.7 67.2 %reduce-scatter.2.cloned.1.call-start = ((), (), s32[]{:S(2)}) async-start(), calls=%async_computation.7 | async-start | bytes 1179648 | tf_op jit(solution)/shard_map/reduce_scatter | solution.py:70
  61.6 1.3 copy-start
  63.6 65.5 %copy-start.20 = (f32[256,256]{1,0:T(8,128)S(1)}, f32[256,256]{1,0:T(8,128)}, u32[]{:S(2)}) copy-start(f32[256,256]{1,0:T(8,128)} %constant.154.clone) | copy-start | bytes 786436
  65.2 64.1 %copy-start.5 = (f32[64,5,256]{2,0,1:T(8,128)S(1)}, f32[64,5,256]{2,0,1:T(8,128)}, u32[]{:S(2)}) copy-start(f32[64,5,256]{2,0,1:T(8,128)} %constant.155.clone) | copy-start | bytes 983044
  65.3 86.8 %copy-start.10 = (s32[1,64,128]{2,1,0:T(8,128)S(1)}, s32[1,64,128]{2,1,0:T(8,128)}, u32[]{:S(2)}) copy-start(s32[1,64,128]{2,1,0:T(8,128)} %param.16) | copy-start | bytes 98308
  98.8 53.3 %copy-start.8 = (f32[8,1,64,128]{3,2,1,0:T(8,128)S(1)}, f32[8,1,64,128]{3,2,1,0:T(8,128)}, u32[]{:S(2)}) copy-start(f32[8,1,64,128]{3,2,1,0:T(8,128)} %param.17) | copy-start | bytes 786436
  99.6 29.4 %all-to-all-start.3 = ((f32[64,4,128]{2,1,0:T(4,128)}), f32[64,4,128]{2,1,0:T(4,128)S(1)}, u32[]{:S(2)}, u32[]{:S(2)}) async-start(f32[64,4,128]{2,1,0:T(4,128)} %bitcast.43), calls=%async_computation.4 | async-start | bytes 262144 | tf_op jit(solution)/shard_map/all_to_all | solution.py:75
  114.0 95.6 %all-gather.3.cloned.1.call-start = ((), (), s32[]{:S(2)}) async-start(), calls=%async_computation.8 | async-start | bytes 1474560 | tf_op jit(solution)/shard_map/all_gather | solution.py:92
  153.1 19.7 %all-to-all-start.2 = ((f32[64,1,144]{2,1,0:T(1,128)}), f32[64,1,144]{2,1,0:T(1,128)}, u32[]{:S(2)}, u32[]{:S(2)}) async-start(f32[64,1,144]{2,1,0:T(1,128)} %copy.71), calls=%async_computation.2 | async-start | bytes 131072 | tf_op jit(solution)/shard_map/all_to_all | solution.py:53
  201.0 2.1 copy-start.3
  203.1 6.5 %copy-start.9 = (f32[2,128,256,1]{2,1,0,3:T(8,128)S(1)}, f32[2,128,256,1]{2,1,0,3:T(8,128)}, u32[]{:S(2)}) copy-start(f32[2,128,256,1]{2,1,0,3:T(8,128)} %constant.175) | copy-start | bytes 786436
  204.9 29.4 %all-to-all-start.1 = ((f32[64,2,2,4,128]{4,3,1,2,0:T(4,128)}), f32[64,2,2,4,128]{4,3,1,2,0:T(4,128)S(1)}, u32[]{:S(2)}, u32[]{:S(2)}) async-start(f32[64,2,2,4,128]{4,3,1,2,0:T(4,128)} %copy.67), calls=%async_computation.1 | async-start | bytes 1048576 | tf_op jit(solution)/shard_map/all_to_all | solution.py:101
  211.6 1.0 copy-start.6
  211.6 1.0 copy-start.7
  211.6 1.0 copy-start.11
  211.6 1.0 copy-start.12
  211.6 1.0 copy-start.13
  211.7 1.0 copy-start.14
  211.7 1.0 copy-start.18
  212.7 5.0 %copy-start.15 = (f32[1024]{0:T(1024)S(1)}, f32[1024]{0:T(1024)}, u32[]{:S(2)}) copy-start(f32[1024]{0:T(1024)} %broadcast_in_dim.211) | copy-start | bytes 12292
  212.7 5.0 %copy-start.16 = (f32[1024]{0:T(1024)S(1)}, f32[1024]{0:T(1024)}, u32[]{:S(2)}) copy-start(f32[1024]{0:T(1024)} %broadcast_in_dim.209) | copy-start | bytes 12292
  212.7 5.0 %copy-start.17 = (s32[1024]{0:T(1024)S(1)}, s32[1024]{0:T(1024)}, u32[]{:S(2)}) copy-start(s32[1024]{0:T(1024)} %get-tuple-element.23) | copy-start | bytes 12292
  217.7 27.1 %copy-start.2 = (f32[2,64,4,2,128,1]{4,1,2,0,3,5:T(8,128)S(1)}, f32[2,64,4,2,128,1]{4,1,2,0,3,5:T(8,128)}, u32[]{:S(2)}) copy-start(f32[2,64,4,2,128,1]{4,1,2,0,3,5:T(8,128)} %constant.173) | copy-start | bytes 1572868
  222.6 60.6 %copy-start.19 = (s32[1,64]{1,0:T(1,128)S(1)}, s32[1,64]{1,0:T(1,128)}, u32[]{:S(2)}) copy-start(s32[1,64]{1,0:T(1,128)} %param.18) | copy-start | bytes 772
  234.2 23.9 %all-to-all-start.5 = ((f32[64,1,16]{2,1,0:T(1,128)}), f32[64,1,16]{2,1,0:T(1,128)S(1)}, u32[]{:S(2)}, u32[]{:S(2)}) async-start(f32[64,1,16]{2,1,0:T(1,128)} %bitcast.54), calls=%async_computation.6 | async-start | bytes 65536 | tf_op jit(solution)/shard_map/all_to_all | solution.py:122
Sparse Core Ops, SparseCore 0:
  65.4 32.4 reduce-scatter.1
  152.2 31.3 all-gather.2

commit v2 on v1

v2 whole, which is shorter than its diff:
```python
import math

import jax
import jax.numpy as jnp
import ml_dtypes
import numpy as np
from jax import lax
from jax.experimental import pallas as pl
from jax.experimental.pallas import tpu as pltpu
from jax.sharding import PartitionSpec as P

HARTREE_SCALE = 200.0
MESH = pl.DeviceIdType.MESH
F32 = jnp.float32
BF16 = jnp.bfloat16

NG = 256
WG = 128
BANDS = 8
TILES = 64
SLAB = 4
CAP = 128
PER = NG // BANDS
SRC = TILES // BANDS
SCALE_IN = float(WG) ** -1.5
SCALE_OUT = float(WG) ** 1.5 / float(NG) ** 3


def halves_of(table):
    high = np.asarray(table, np.float64).astype(ml_dtypes.bfloat16)
    low = (table - high.astype(np.float64)).astype(ml_dtypes.bfloat16)
    return np.stack([high, low])


def tables():
    position = np.arange(NG)
    modes = np.arange(WG) - WG // 2
    angle = (np.outer(position, modes) % NG) * (2.0 * math.pi / NG)
    cosine, sine = np.cos(angle), np.sin(angle)
    wave = np.stack([np.stack([cosine, -sine], 1), np.stack([sine, cosine], 1)], 0)
    wave_y = wave.reshape(2, TILES, SLAB, 2, WG).transpose(1, 0, 2, 3, 4).reshape(2 * NG, 2 * WG)
    wave_x = wave.reshape(2, NG, 2, TILES, 2).transpose(0, 1, 2, 4, 3).reshape(2 * NG, 2 * WG)
    wave_z = wave.transpose(2, 3, 0, 1).reshape(2 * WG, 2 * NG)
    angle = lambda n: (np.outer(n, position) % NG) * (2.0 * math.pi / NG)
    rows = np.concatenate([np.cos(angle(np.arange(NG // 2 + 1))), np.sin(angle(np.arange(1, NG // 2)))])
    basis = rows / np.sqrt(np.sum(rows * rows, axis=1, keepdims=True))
    basis_y = basis.reshape(NG, TILES, SLAB).transpose(0, 2, 1).reshape(NG, NG)
    planes = (np.arange(TILES)[:, None] * SLAB + np.arange(8)[None, :]) % NG
    back_y = basis.T[planes] * (np.arange(8) <= SLAB)[None, :, None]
    named = dict(
        wave_y=wave_y,
        wave_x=wave_x,
        wave_z=wave_z,
        basis_t=basis.T,
        basis=basis,
        basis_y=basis_y,
        back_y=back_y.reshape(8 * TILES, NG),
        wave_zt=wave_z.T,
        wave_xt=wave_x.T,
        wave_yt=wave_y.T,
    )
    return {name: halves_of(table) for name, table in named.items()}


LATE = ("wave_x", "wave_z", "basis_t", "basis", "wave_zt", "wave_xt", "basis_y", "back_y", "wave_yt")


def split(value):
    high = value.astype(BF16)
    return high, (value - high.astype(F32)).astype(BF16)


def dot3(left, right, last=False):
    dims = (((1,), (1 if last else 0,)), ((), ()))
    one = lambda a, b: lax.dot_general(a, b, dims, preferred_element_type=F32)
    return one(left[0], right[0]) + (one(left[0], right[1]) + one(left[1], right[0]))


def pair(ref):
    return ref[0], ref[1]


def iota(shape, dim):
    return lax.broadcasted_iota(jnp.int32, shape, dim)


def as_column(row):
    size = row.shape[1]
    on = iota((size, size), 0) == iota((size, size), 1)
    return jnp.sum(jnp.where(on, jnp.broadcast_to(row, (size, size)), 0.0), axis=1, keepdims=True)


def drain(ref, sem):
    pltpu.make_async_copy(ref, ref, sem).wait()


def kernel(
    coef, half, occupation, count, wave_y,
    potential, corner, weight, wave_x_h, wave_z_h, basis_t_h, basis_h, wave_zt_h, wave_xt_h,
    basis_y_h, back_y_h, wave_yt_h,
    action, fit,
    wave_x, wave_z, basis_t, basis, wave_zt, wave_xt, basis_y, back_y, wave_yt,
    pot, corn, weig,
    s1, r1, s2, r2, bx, lz, psi, ez, sr, rs1, rs2, ss, ys, sb, g, green, pk, pr, wst, ht, stage, o, f,
    load_sem, a1, a2, pt_s, pt_r, t1_s, t1_r, t2_s, t2_r, sf, bk, g1_s, g1_r, g2_s, g2_r, fin,
):
    b = lax.axis_index("band")
    p = lax.axis_index("pw")
    x, c = b // 2, b % 2
    partner = b + 1 - 2 * c
    heavy = p // SRC == b

    loads = []
    for j in range(SLAB):
        loads.append((potential.at[:, j, :], pot.at[j]))
    for source, target in (
        (corner, corn), (weight, weig), (wave_x_h, wave_x), (wave_z_h, wave_z), (basis_t_h, basis_t), (basis_h, basis),
        (wave_zt_h, wave_zt), (wave_xt_h, wave_xt), (basis_y_h, basis_y), (back_y_h, back_y), (wave_yt_h, wave_yt),
    ):
        loads.append((source, target))
    loads = [pltpu.make_async_copy(a, z, load_sem.at[n]) for n, (a, z) in enumerate(loads)]
    for load in loads:
        load.start()

    barrier = pltpu.get_barrier_semaphore()

    def greet_pw(k, _):
        pl.semaphore_signal(barrier, inc=1, device_id={"pw": lax.rem(p + k, TILES)}, device_id_type=MESH)
        return 0

    lax.fori_loop(1, TILES, greet_pw, 0)

    def greet_band(k, _):
        pl.semaphore_signal(barrier, inc=1, device_id={"band": lax.rem(b + k, BANDS)}, device_id_type=MESH)
        return 0

    lax.fori_loop(1, BANDS, greet_band, 0)

    def greet_fit(q, _):
        @pl.when(jnp.logical_not(jnp.logical_and(heavy, q == p)))
        def _():
            pl.semaphore_signal(barrier, inc=1, device_id={"band": p // SRC, "pw": q}, device_id_type=MESH)
        return 0

    lax.fori_loop(0, TILES, greet_fit, 0)

    lane = iota((WG, WG), 1)
    masks = []
    for i in range(2):
        reach = as_column(half[i : i + 1, :].astype(F32))
        masks.append(jnp.where(jnp.abs(lane - WG // 2).astype(F32) <= reach, 1.0, 0.0))
    rows = [
        jnp.concatenate([coef[0, k, i] * (masks[i] * SCALE_IN) for i in range(2)], axis=1) for k in range(2)
    ]
    section = dot3(pair(wave_y), split(jnp.concatenate(rows, axis=0)))
    for i in range(2):
        s1[:, i] = section[:, i * WG : (i + 1) * WG].reshape(TILES, 8, WG)

    @pl.when(heavy)
    def _():
        pl.semaphore_wait(barrier, TILES - 1 + BANDS - 1 + TILES - 1)

    @pl.when(jnp.logical_not(heavy))
    def _():
        pl.semaphore_wait(barrier, TILES - 1 + BANDS - 1 + TILES)

    def exchange(source, target, sems):
        def send(k, _):
            q = lax.rem(p + k, TILES)
            pltpu.make_async_remote_copy(
                source(q), target(p), sems.at[0], sems.at[1], device_id={"pw": q}, device_id_type=MESH
            ).start()
            return 0

        lax.fori_loop(1, TILES, send, 0)

    exchange(lambda q: s1.at[q], lambda q: r1.at[q], a1)
    r1[p] = s1[p]

    loads[SLAB].wait()
    loads[SLAB + 1].wait()

    @pl.when(heavy)
    def _():
        flat = pk.reshape(TILES * 16, CAP)
        for k in range(8):
            flat[pl.ds(k, TILES, stride=16), :] = weig[k, 0]
        flat[pl.ds(8, TILES, stride=16), :] = corn[0].astype(F32)

    mode = lambda k: jnp.where(k <= NG // 2, k, k - NG // 2)
    n_y = mode(iota((NG, CAP), 0))
    n_z = mode((p // PER) * CAP + iota((NG, CAP), 1))
    n_x = mode(b * PER + lax.rem(p, PER))
    square = n_y * n_y + n_z * n_z + n_x * n_x
    green[...] = jnp.where(square > 0, HARTREE_SCALE / jnp.maximum(square, 1).astype(F32), 0.0)

    for load in loads[:SLAB] + loads[SLAB + 2 :]:
        load.wait()

    drain(r1.at[pl.ds(0, TILES - 1)], a1.at[1])

    @pl.when(heavy)
    def _():
        def send(k, _):
            q = lax.rem(p + k, TILES)
            pltpu.make_async_remote_copy(
                pk.at[q, pl.ds(0, 9)], pr.at[p % SRC, pl.ds(0, 9)], pt_s, pt_r.at[p % SRC],
                device_id={"pw": q}, device_id_type=MESH,
            ).start()
            return 0

        lax.fori_loop(1, TILES, send, 0)
        pr[p % SRC, 0:9] = pk[p, 0:9]

    flat = r1.reshape(TILES * 16, WG)
    for k in range(2):
        for i in range(2):
            for j in range(SLAB):
                high, low = split(flat[pl.ds(i * 8 + k * SLAB + j, TILES, stride=16), :])
                at = (pl.ds(k * WG + i * TILES, TILES), pl.ds(j * WG, WG))
                bx[(0,) + at] = high
                bx[(1,) + at] = low
    turned = dot3(pair(wave_x), pair(bx))
    for j in range(SLAB):
        for k in range(2):
            high, low = split(turned[k * NG : (k + 1) * NG, j * WG : (j + 1) * WG])
            lz[j, 0, :, k * WG : (k + 1) * WG] = high
            lz[j, 1, :, k * WG : (k + 1) * WG] = low

    corner_on = jnp.logical_and(iota((NG, NG), 0) == 0, iota((NG, NG), 1) == 0)

    def density_step(j, _):
        orbital = dot3((lz[j, 0], lz[j, 1]), pair(wave_z))
        psi[j] = orbital
        real, imag = orbital[:, :NG], orbital[:, NG:]
        density = occupation[0] * (real * real + imag * imag)
        mean = jnp.sum(jnp.sum(density, axis=0, keepdims=True), axis=1, keepdims=True) * (1.0 / (NG * NG))
        modes = dot3(split(density - mean), pair(basis_t))
        modes = dot3(pair(basis), split(modes))
        modes = modes + jnp.where(corner_on, NG * mean, 0.0)
        sr[j] = modes.reshape(BANDS // 2, 2, PER, NG)
        pltpu.make_async_remote_copy(
            sr.at[j, :, 1 - c], rs1.at[j], t1_s.at[j], t1_r.at[j], device_id={"band": partner}, device_id_type=MESH
        ).start()
        return 0

    lax.fori_loop(0, SLAB, density_step, 0)

    def across(j, _):
        drain(rs1.at[j], t1_r.at[j])
        for k in range(BANDS // 2):
            rs1[j, k] = rs1[j, k] + sr[j, k, c]

        def send(k, _):
            to = lax.rem(x + k, BANDS // 2)
            pltpu.make_async_remote_copy(
                rs1.at[j, to], rs2.at[j, x], t2_s.at[j], t2_r.at[j],
                device_id={"band": 2 * to + c}, device_id_type=MESH,
            ).start()
            return 0

        lax.fori_loop(1, BANDS // 2, send, 0)
        rs2[j, x] = rs1[j, x]
        return 0

    lax.fori_loop(0, SLAB, across, 0)

    def product_step(j, _):
        value = pot[j]
        field = psi[j] * jnp.concatenate([value, value], axis=1)
        ez[j] = dot3(split(field), pair(wave_zt))
        return 0

    lax.fori_loop(0, SLAB, product_step, 0)

    flat_s = ss.reshape(TILES * 8, CAP)

    def gather_bands(j, _):
        drain(rs2.at[j, pl.ds(0, BANDS // 2 - 1)], t2_r.at[j])
        total = (rs2[j, 0] + rs2[j, 1]) + (rs2[j, 2] + rs2[j, 3])
        for h in range(2):
            flat_s[pl.ds(h * PER * 8 + j, PER, stride=8), :] = total[:, h * CAP : (h + 1) * CAP]
        return 0

    for j in range(SLAB):
        gather_bands(j, 0)

    four = pl.ds(0, SLAB)
    exchange(lambda q: ss.at[q, four], lambda q: ys.at[q, four], sf)
    ys[p, 0:SLAB] = ss[p, 0:SLAB]

    cols = [jnp.concatenate([ez[j, :, k * WG : (k + 1) * WG] for j in range(SLAB)], axis=1) for k in range(2)]
    cube = dot3(pair(wave_xt), split(jnp.concatenate(cols, axis=0)))
    flat = s2.reshape(TILES * 16, WG)
    for k in range(2):
        for i in range(2):
            for j in range(SLAB):
                at = k * WG + i * TILES
                flat[pl.ds(i * 8 + k * SLAB + j, TILES, stride=16), :] = cube[at : at + TILES, j * WG : (j + 1) * WG]

    drain(ys.at[pl.ds(0, TILES - 1), four], sf.at[1])
    flat_y = ys.reshape(TILES * 8, CAP)
    lines = jnp.concatenate([flat_y[pl.ds(j, TILES, stride=8), :] for j in range(SLAB)], axis=0)
    mean = jnp.sum(lines, axis=0, keepdims=True) * (1.0 / NG)
    modes = dot3(pair(basis_y), split(lines - mean))
    modes = modes + jnp.where(iota((NG, CAP), 0) == 0, math.sqrt(NG) * mean, 0.0)
    sb[...] = dot3(pair(back_y), split(modes * green[...])).reshape(TILES, 8, CAP)
    five = pl.ds(0, SLAB + 1)
    exchange(lambda q: sb.at[q, five], lambda q: g.at[b, q, five], bk)
    g[b, p] = sb[p]
    exchange(lambda q: s2.at[q], lambda q: r2.at[q], a2)
    r2[p] = s2[p]

    def point_step(i, _):
        source = SRC * b + i

        @pl.when(source != p)
        def _():
            drain(pr.at[i, pl.ds(0, 9)], pt_r.at[i])

        data = pr[i, 0:9]
        place = data[8:9].astype(jnp.int32)
        at_x = place // (SLAB * NG)
        at_y = lax.rem(place // NG, SLAB)
        across_x = iota((NG, CAP), 0)
        on = [across_x == at_x, across_x == lax.rem(at_x + 1, NG)]
        for y in range(SLAB + 1):
            for dz in range(2):
                value = []
                for dx in range(2):
                    first = jnp.where(at_y == y, data[4 * dx + dz : 4 * dx + dz + 1], 0.0)
                    value.append(jnp.where(at_y == y - 1, data[4 * dx + 2 + dz : 4 * dx + 3 + dz], first))
                value = jnp.where(on[0], value[0], jnp.where(on[1], value[1], 0.0))
                high, low = split(value)
                wst[i, 0, y * NG : (y + 1) * NG, dz * CAP : (dz + 1) * CAP] = high
                wst[i, 1, y * NG : (y + 1) * NG, dz * CAP : (dz + 1) * CAP] = low
        return 0

    lax.fori_loop(0, SRC, point_step, 0)

    drain(g.at[b, pl.ds(0, TILES - 1), five], bk.at[1])

    def pass_on(k):
        block = lax.rem(x + BANDS // 2 - k, BANDS // 2) * 2 + c
        pltpu.make_async_remote_copy(
            g.at[block, :, five], g.at[block, :, five], g2_s.at[k], g2_r.at[k],
            device_id={"band": partner}, device_id_type=MESH,
        ).start()

    def send_x(k, _):
        to = lax.rem(x + k, BANDS // 2)
        pltpu.make_async_remote_copy(
            g.at[b, :, five], g.at[b, :, five], g1_s.at[k], g1_r.at[k],
            device_id={"band": 2 * to + c}, device_id_type=MESH,
        ).start()
        return 0

    lax.fori_loop(1, BANDS // 2, send_x, 0)
    pass_on(0)

    def forward(k, _):
        block = lax.rem(x + BANDS // 2 - k, BANDS // 2) * 2 + c
        drain(g.at[block, :, five], g1_r.at[k])
        pass_on(k)
        return 0

    lax.fori_loop(1, BANDS // 2, forward, 0)

    def arrived(k, _):
        block = lax.rem(x + BANDS // 2 - k, BANDS // 2) * 2 + 1 - c
        drain(g.at[block, :, five], g2_r.at[k])
        return 0

    lax.fori_loop(0, BANDS // 2, arrived, 0)

    flat_g = g.reshape(BANDS * TILES * 8, CAP)
    for y in range(SLAB + 1):
        for h in range(2):
            for n in range(BANDS):
                high, low = split(flat_g[pl.ds(n * TILES * 8 + h * PER * 8 + y, PER, stride=8), :])
                stage[0, n * PER : (n + 1) * PER, h * CAP : (h + 1) * CAP] = high
                stage[1, n * PER : (n + 1) * PER, h * CAP : (h + 1) * CAP] = low
        plane = dot3(pair(basis_t), pair(stage))
        plane = dot3(pair(basis_t), split(plane), last=True)
        high, low = split(plane)
        ht[0, :, y * NG : (y + 1) * NG] = high
        ht[1, :, y * NG : (y + 1) * NG] = low

    def fit_step(i, _):
        lines = dot3(pair(ht), (wst[i, 0], wst[i, 1]))
        at_z = lax.rem(pr[i, 8:9].astype(jnp.int32), NG)
        at_z = jnp.concatenate([at_z, lax.rem(at_z + 1, NG)], axis=1)
        lines = jnp.sum(jnp.where(iota((NG, 2 * CAP), 0) == at_z, lines, 0.0), axis=0, keepdims=True)
        o[i] = lines[:, :CAP] + lines[:, CAP:]
        return 0

    lax.fori_loop(0, SRC, fit_step, 0)

    def fit_send(n, _):
        to, i = n // SRC, lax.rem(n, SRC)

        @pl.when(jnp.logical_not(jnp.logical_and(to == b, SRC * b + i == p)))
        def _():
            pltpu.make_async_remote_copy(
                o.at[i], f.at[p], fin.at[0], fin.at[1],
                device_id={"band": to, "pw": SRC * b + i}, device_id_type=MESH,
            ).start()
        return 0

    lax.fori_loop(0, BANDS * SRC, fit_send, 0)

    @pl.when(heavy)
    def _():
        f[p] = o[p % SRC]

    drain(r2.at[pl.ds(0, TILES - 1)], a2.at[1])
    cube = jnp.concatenate([r2[:, i].reshape(TILES * 8, WG) for i in range(2)], axis=1)
    cube = dot3(pair(wave_yt), split(cube))
    for k in range(2):
        for i in range(2):
            action[0, k, i] = cube[k * WG : (k + 1) * WG, i * WG : (i + 1) * WG] * (masks[i] * SCALE_OUT)

    @pl.when(heavy)
    def _():
        drain(f.at[pl.ds(0, TILES - 1)], fin.at[1])
        drain(f.at[pl.ds(0, TILES - 1)], fin.at[0])

    @pl.when(jnp.logical_not(heavy))
    def _():
        drain(f, fin.at[1])
        drain(f, fin.at[0])

    live = iota((TILES, CAP), 1).astype(F32) < as_column(count[...].astype(F32))
    fit[0] = jnp.where(live, f[...].reshape(TILES, CAP), 0.0)

    drain(s1.at[pl.ds(0, TILES - 1)], a1.at[0])
    drain(s2.at[pl.ds(0, TILES - 1)], a2.at[0])
    drain(ss.at[pl.ds(0, TILES - 1), four], sf.at[0])
    drain(sb.at[pl.ds(0, TILES - 1), five], bk.at[0])

    @pl.when(heavy)
    def _():
        drain(pk.at[pl.ds(0, TILES - 1), pl.ds(0, 9)], pt_s)

    def sent(j, _):
        drain(rs1.at[j], t1_s.at[j])
        drain(rs1.at[j, pl.ds(0, BANDS // 2 - 1)], t2_s.at[j])
        return 0

    lax.fori_loop(0, SLAB, sent, 0)

    def passed(k, _):
        drain(g.at[b, :, five], g2_s.at[k])

        @pl.when(k > 0)
        def _():
            drain(g.at[b, :, five], g1_s.at[k])
        return 0

    lax.fori_loop(0, BANDS // 2, passed, 0)


def body(coefficients, halfwidth, occupation, potential, corner, weight, count):
    held = {name: jnp.asarray(table) for name, table in tables().items()}
    late = [held[name] for name in LATE]
    vmem = pl.BlockSpec(memory_space=pltpu.VMEM)
    anywhere = pl.BlockSpec(memory_space=pl.ANY)
    dma = pltpu.SemaphoreType.DMA
    block = lambda *shape: pltpu.VMEM(shape, F32)
    short = lambda *shape: pltpu.VMEM(shape, BF16)
    scratch = [short(*table.shape) for table in late]
    scratch += [
        block(SLAB, NG, NG),
        pltpu.VMEM((1, TILES, CAP), jnp.int32),
        block(8, 1, TILES, CAP),
        block(TILES, 2, 8, WG),
        block(TILES, 2, 8, WG),
        block(TILES, 2, 8, WG),
        block(TILES, 2, 8, WG),
        short(2, 2 * WG, SLAB * WG),
        short(SLAB, 2, NG, 2 * WG),
        block(SLAB, NG, 2 * NG),
        block(SLAB, NG, 2 * WG),
        block(SLAB, BANDS // 2, 2, PER, NG),
        block(SLAB, BANDS // 2, PER, NG),
        block(SLAB, BANDS // 2, PER, NG),
        block(TILES, 8, CAP),
        block(TILES, 8, CAP),
        block(TILES, 8, CAP),
        block(BANDS, TILES, 8, CAP),
        block(NG, CAP),
        block(TILES, 16, CAP),
        block(SRC, 16, CAP),
        short(SRC, 2, (SLAB + 1) * NG, 2 * CAP),
        short(2, NG, (SLAB + 1) * NG),
        short(2, NG, NG),
        block(SRC, 1, CAP),
        block(TILES, 1, CAP),
    ]
    scratch += [
        dma((SLAB + 2 + len(late),)),
        dma((2,)), dma((2,)),
        dma(()), dma((SRC,)),
        dma((SLAB,)), dma((SLAB,)), dma((SLAB,)), dma((SLAB,)),
        dma((2,)), dma((2,)),
        dma((BANDS // 2,)), dma((BANDS // 2,)), dma((BANDS // 2,)), dma((BANDS // 2,)),
        dma((2,)),
    ]
    return pl.pallas_call(
        kernel,
        out_shape=(
            jax.ShapeDtypeStruct(coefficients.shape, F32),
            jax.ShapeDtypeStruct(corner.shape, F32),
        ),
        in_specs=[vmem, vmem, pl.BlockSpec(memory_space=pltpu.SMEM), vmem, vmem] + [anywhere] * (3 + len(late)),
        out_specs=(vmem, vmem),
        scratch_shapes=scratch,
        compiler_params=pltpu.CompilerParams(
            collective_id=0, has_side_effects=True, vmem_limit_bytes=52 * 1024 * 1024
        ),
    )(coefficients, halfwidth, occupation, count, held["wave_y"], potential, corner, weight, *late)


def solution(mesh):
    placed = (
        P("band", None, "pw", None, None),
        P("pw", None),
        P("band"),
        P(None, "pw", None),
        P("pw", None, None),
        P(None, "pw", None, None),
        P("pw", None),
    )
    return jax.shard_map(
        body,
        mesh=mesh,
        in_specs=placed,
        out_specs=(P("band", None, "pw", None, None), P("pw", None, None)),
        check_vma=False,
    )
```

time: 293 us -> 121 us (0.41)
  Pallas kernels: 0 us -> 112 us
  waiting for transfers between devices: 110 us -> 0 us
  starting transfers between devices: 54.9 us -> 0 us
  blocking collectives: 46.6 us -> 0 us
  local copies, waits for them, and re-layouts: 34.7 us -> 6.83 us
  matrix products: 22.2 us -> 0 us
  between operations: 16.5 us -> 1.35 us
  other arithmetic: 6.09 us -> 0 us
    pallas_call x0 -> x1, Pallas kernels: none -> 112 us  [body(): pl.pallas_call(kernel, out_shape=(jax.ShapeDtypeStruct(coefficients.shape...]
    all_to_all x5 -> x0, waiting for transfers between devices: 77.1 us -> none  [the longest x1 29.2 us: body(): section = lax.all_to_all(section, 'pw', 0, 0, tiled=True)]
    all_to_all x5 -> x0, starting transfers between devices: 54.8 us -> none  [the longest x1 19.3 us: body(): section = lax.all_to_all(section, 'pw', 0, 0, tiled=True)]
    reduce_scatter x1 -> x0, waiting for transfers between devices: 32.7 us -> none  [body(): lax.psum_scatter(spectrum, 'band', scatter_dimension=0, tiled=True)]
    all_gather x1 -> x0, blocking collectives: 25 us -> none  [body(): total = lax.all_gather(total, 'band', axis=1, tiled=True)]
    dot_general x14 -> x0, matrix products: 22.2 us -> none  [dot(): jnp.einsum(spec, *operands, precision=HIGH, preferred_element_type=jnp.fl...]
    all_to_all x1 -> x0, blocking collectives: 21.5 us -> none  [body(): spectrum = lax.all_to_all(spectrum, 'pw', 0, 0, tiled=True)]
    broadcast_in_dim x8 -> x0, local copies, waits for them, and re-layouts: 10.2 us -> none  [body(): column = column + jnp.where(at_y[:, None] & at_x[None], w[None, None], 0.0)]
  transfers between devices with their start and end apart: 7 -> 0, of which waited for: 6 -> 0; matrix products, arithmetic and copies ran while one was open for 17% -> 0% of each run, Pallas kernels for 0% -> 0%
where the time goes in v2:
time: 121 us
  Pallas kernels  112 us (93%)
  local copies, waits for them, and re-layouts  6.83 us (6%)
  between operations  1.35 us (1%)
    pallas_call x1, Pallas kernels, body(): pl.pallas_call(kernel, out_shape=(jax.ShapeDtypeStruct(coefficients.shape...  112 us
    unnamed x18, local copies, waits for them, and re-layouts  6.83 us

profile of v2, /device:TPU:1, one launch (start us, length us, event | category | flops | bytes accessed | tf_op | source)
XLA Modules:
  0.0 120.7 jit_solution(1315510752965773799)
XLA Ops:
  0.6 0.0 copy-start.7
  0.6 0.0 copy-start.6
  1.3 0.0 copy-done.7
  1.3 0.0 copy-done.6
  1.3 0.0 copy-start
  1.3 0.9 copy-done
  2.3 0.0 copy-start.1
  2.3 0.9 copy-done.1
  3.2 0.0 copy-start.2
  3.2 0.9 copy-done.2
  4.2 0.0 copy-start.3
  4.2 0.9 copy-done.3
  5.1 0.0 copy-start.4
  5.1 0.9 copy-done.4
  6.1 0.0 copy-start.5
  6.1 0.8 copy-done.5
  6.8 112.5 %shard_map.176 = (f32[1,2,2,128,128]{4,3,2,1,0:T(8,128)S(1)}, f32[1,64,128]{2,1,0:T(8,128)S(1)}) custom-call(f32[1,2,2,128,128]{4,3,2,1,0:T(8,128)S(1)} %copy-done, s32[2,128]{1,0:T(2,128)S(1)} %copy-done.6, f32[1]{0:T(128)S(6)} %copy.21.occupation, s32[1,64]{1,0:T(1,128)S(1)} %copy-done.7, bf16[2,512,256]{2,1,0:T(8,128)(2,1)} %constant.20.clone.wave_y, ...), custom_call_target="tpu_custom_call" | custom-call | tf_op jit(solution)/shard_map/pallas_call | solution.py:509
  119.4 0.7 copy.22
  120.1 0.6 copy.23
Async XLA Ops:
  0.6 0.7 copy-start.7
  0.6 0.7 copy-start.6
  1.3 1.0 copy-start
  2.3 0.9 copy-start.1
  3.2 0.9 copy-start.2
  4.2 0.9 copy-start.3
  5.1 0.9 copy-start.4
  6.1 0.8 copy-start.5

commit v3 on v2

v3 whole, which is shorter than its diff:
```python
import math

import jax
import jax.numpy as jnp
import ml_dtypes
import numpy as np
from jax import lax
from jax.experimental import pallas as pl
from jax.experimental.pallas import tpu as pltpu
from jax.sharding import PartitionSpec as P

HARTREE_SCALE = 200.0
MESH = pl.DeviceIdType.MESH
F32 = jnp.float32
BF16 = jnp.bfloat16

NG = 256
WG = 128
BANDS = 8
TILES = 64
SLAB = 4
CAP = 128
PER = NG // BANDS
SRC = TILES // BANDS
GROUPS = (pl.ds(0, 3), pl.ds(3, 2))
SCALE_IN = float(WG) ** -1.5
SCALE_OUT = float(WG) ** 1.5 / float(NG) ** 3


def halves_of(table):
    high = np.asarray(table, np.float64).astype(ml_dtypes.bfloat16)
    low = (table - high.astype(np.float64)).astype(ml_dtypes.bfloat16)
    return np.stack([high, low])


def tables():
    position = np.arange(NG)
    modes = np.arange(WG) - WG // 2
    angle = (np.outer(position, modes) % NG) * (2.0 * math.pi / NG)
    cosine, sine = np.cos(angle), np.sin(angle)
    wave = np.stack([np.stack([cosine, -sine], 1), np.stack([sine, cosine], 1)], 0)
    wave_y = wave.reshape(2, TILES, SLAB, 2, WG).transpose(1, 2, 0, 3, 4).reshape(2 * NG, 2 * WG)
    wave_x = wave.reshape(2, NG, 2, TILES, 2).transpose(0, 1, 2, 4, 3).reshape(2 * NG, 2 * WG)
    wave_z = wave.transpose(2, 3, 0, 1).reshape(2 * WG, 2 * NG)
    angle = lambda n: (np.outer(n, position) % NG) * (2.0 * math.pi / NG)
    rows = np.concatenate([np.cos(angle(np.arange(NG // 2 + 1))), np.sin(angle(np.arange(1, NG // 2)))])
    basis = rows / np.sqrt(np.sum(rows * rows, axis=1, keepdims=True))
    basis_y = basis.reshape(NG, TILES, SLAB).transpose(0, 2, 1).reshape(NG, NG)
    planes = (np.arange(TILES)[None, :] * SLAB + np.arange(SLAB + 1)[:, None]) % NG
    named = dict(
        wave_y=wave_y,
        wave_x=wave_x,
        wave_z=wave_z,
        basis_t=basis.T,
        basis=basis,
        basis_y=basis_y,
        back_y=basis.T[planes.reshape(-1)],
        wave_zt=wave_z.T,
        wave_xt=wave_x.T,
        wave_yt=wave_y.T,
    )
    return {name: halves_of(table) for name, table in named.items()}


LATE = ("wave_y", "wave_x", "wave_z", "basis_t", "basis", "wave_zt", "wave_xt", "basis_y", "back_y", "wave_yt")


def split(value):
    high = value.astype(BF16)
    return high, (value - high.astype(F32)).astype(BF16)


def dot(left, right):
    return jnp.dot(left, right, preferred_element_type=F32)


def dot3(left, right):
    return dot(left[0], right[0]) + (dot(left[0], right[1]) + dot(left[1], right[0]))


def pair(ref):
    return ref[0], ref[1]


def iota(shape, dim):
    return lax.broadcasted_iota(jnp.int32, shape, dim)


def as_column(row):
    size = row.shape[1]
    on = iota((size, size), 0) == iota((size, size), 1)
    return jnp.sum(jnp.where(on, jnp.broadcast_to(row, (size, size)), 0.0), axis=1, keepdims=True)


def drain(ref, sem):
    pltpu.make_async_copy(ref, ref, sem).wait()


def kernel(
    half, occupation, count,
    coef_h, wave_y_h, potential, corner, weight, wave_x_h, wave_z_h, basis_t_h, basis_h, wave_zt_h, wave_xt_h,
    basis_y_h, back_y_h, wave_yt_h,
    action, fit,
    wave_y, wave_x, wave_z, basis_t, basis, wave_zt, wave_xt, basis_y, back_y, wave_yt,
    coef, pot, corn, weig,
    s1, r1, s2, r2, psi, sr, rs1, rs2, ss, ys, sb, g, green, pk, pr, wst, pick, part, o, f,
    load_sem, a1_s, a1_r, a2, pt_s, pt_r, t1_s, t1_r, t2_s, t2_r, sf, bk_s, bk_r, g1_s, g1_r, g2_s, g2_r, fin,
):
    b = lax.axis_index("band")
    p = lax.axis_index("pw")
    x, c = b // 2, b % 2
    chips = BANDS // 2
    partner = b + 1 - 2 * c
    heavy = p // SRC == b
    others = pl.ds(0, TILES - 1)

    loads = [(coef_h, coef), (wave_y_h, wave_y)]
    for j in range(SLAB):
        loads.append((potential.at[:, j, :], pot.at[j]))
    for source, target in (
        (corner, corn), (weight, weig), (wave_x_h, wave_x), (wave_z_h, wave_z), (basis_t_h, basis_t), (basis_h, basis),
        (wave_zt_h, wave_zt), (wave_xt_h, wave_xt), (basis_y_h, basis_y), (back_y_h, back_y), (wave_yt_h, wave_yt),
    ):
        loads.append((source, target))
    loads = [pltpu.make_async_copy(a, z, load_sem.at[n]) for n, (a, z) in enumerate(loads)]
    loads[0].start()
    loads[1].start()

    barrier = pltpu.get_barrier_semaphore()

    def greet_pw(k, _):
        pl.semaphore_signal(barrier, inc=1, device_id={"pw": lax.rem(p + k, TILES)}, device_id_type=MESH)
        return 0

    lax.fori_loop(1, TILES, greet_pw, 0)

    def greet_fit(q, _):
        @pl.when(jnp.logical_not(jnp.logical_and(heavy, q == p)))
        def _():
            pl.semaphore_signal(barrier, inc=1, device_id={"band": p // SRC, "pw": q}, device_id_type=MESH)
        return 0

    lax.fori_loop(0, TILES, greet_fit, 0)

    def greet_band(k, _):
        pl.semaphore_signal(barrier, inc=1, device_id={"band": lax.rem(b + k, BANDS)}, device_id_type=MESH)
        return 0

    lax.fori_loop(1, BANDS, greet_band, 0)
    for load in loads[2:]:
        load.start()

    lane = iota((WG, WG), 1)
    masks = []
    for i in range(2):
        reach = as_column(half[i : i + 1, :].astype(F32))
        masks.append(jnp.where(jnp.abs(lane - WG // 2).astype(F32) <= reach, 1.0, 0.0))
    loads[0].wait()
    loads[1].wait()
    loads = loads[2:]
    rows = [
        jnp.concatenate([coef[0, k, i] * (masks[i] * SCALE_IN) for i in range(2)], axis=1) for k in range(2)
    ]
    section = dot3(pair(wave_y), split(jnp.concatenate(rows, axis=0)))
    flat_s1 = s1.reshape(TILES * 16, WG)
    for i in range(2):
        flat_s1[pl.ds(i, 2 * NG, stride=2), :] = section[:, i * WG : (i + 1) * WG]
    r1[p] = s1[p]

    @pl.when(heavy)
    def _():
        pl.semaphore_wait(barrier, TILES - 1 + BANDS - 1 + TILES - 1)

    @pl.when(jnp.logical_not(heavy))
    def _():
        pl.semaphore_wait(barrier, TILES - 1 + BANDS - 1 + TILES)

    def exchange(source, target, send_sem, recv_sem):
        def send(k, _):
            q = lax.rem(p + k, TILES)
            pltpu.make_async_remote_copy(
                source(q), target(p), send_sem, recv_sem, device_id={"pw": q}, device_id_type=MESH
            ).start()
            return 0

        lax.fori_loop(1, TILES, send, 0)

    plane_rows = [pl.ds(4 * j, 4) for j in range(SLAB)]
    for j in range(SLAB):
        exchange(lambda q: s1.at[q, plane_rows[j]], lambda q: r1.at[q, plane_rows[j]], a1_s, a1_r.at[j])

    loads[SLAB].wait()
    loads[SLAB + 1].wait()

    @pl.when(heavy)
    def _():
        flat = pk.reshape(TILES * 16, CAP)
        for k in range(8):
            flat[pl.ds(k, TILES, stride=16), :] = weig[k, 0]
        flat[pl.ds(8, TILES, stride=16), :] = corn[0].astype(F32)

    mode = lambda k: jnp.where(k <= NG // 2, k, k - NG // 2)
    n_y = mode(iota((NG, CAP), 0))
    n_z = mode((p // PER) * CAP + iota((NG, CAP), 1))
    n_x = mode(b * PER + lax.rem(p, PER))
    square = n_y * n_y + n_z * n_z + n_x * n_x
    green[...] = jnp.where(square > 0, HARTREE_SCALE / jnp.maximum(square, 1).astype(F32), 0.0)

    for load in loads[:SLAB] + loads[SLAB + 2 :]:
        load.wait()

    corner_on = jnp.logical_and(iota((NG, NG), 0) == 0, iota((NG, NG), 1) == 0)
    flat_r1 = r1.reshape(TILES * 16, WG)

    def density_step(j):
        drain(r1.at[others, plane_rows[j]], a1_r.at[j])
        rows = [flat_r1[pl.ds(4 * j + n, TILES, stride=16), :] for n in range(4)]
        turned = dot3(pair(wave_x), split(jnp.concatenate(rows, axis=0)))
        turned = jnp.concatenate([turned[:NG], turned[NG:]], axis=1)
        orbital = dot3(split(turned), pair(wave_z))
        psi[j] = orbital
        real, imag = orbital[:, :NG], orbital[:, NG:]
        density = occupation[0] * (real * real + imag * imag)
        mean = jnp.sum(jnp.sum(density, axis=0, keepdims=True), axis=1, keepdims=True) * (1.0 / (NG * NG))
        modes = dot3(split(density - mean), pair(basis_t))
        modes = dot3(pair(basis), split(modes))
        modes = modes + jnp.where(corner_on, NG * mean, 0.0)
        sr[j] = modes.reshape(chips, 2, PER, NG)
        pltpu.make_async_remote_copy(
            sr.at[j, :, 1 - c], rs1.at[j], t1_s.at[j], t1_r.at[j], device_id={"band": partner}, device_id_type=MESH
        ).start()

    def across(j):
        drain(rs1.at[j], t1_r.at[j])
        for k in range(chips):
            rs1[j, k] = rs1[j, k] + sr[j, k, c]

        def send(k, _):
            to = lax.rem(x + k, chips)
            pltpu.make_async_remote_copy(
                rs1.at[j, to], rs2.at[j, x], t2_s.at[j], t2_r.at[j],
                device_id={"band": 2 * to + c}, device_id_type=MESH,
            ).start()
            return 0

        lax.fori_loop(1, chips, send, 0)
        rs2[j, x] = rs1[j, x]

    flat_ss = ss.reshape(SLAB * TILES, CAP)

    def gather_bands(j):
        drain(rs2.at[j, pl.ds(0, chips - 1)], t2_r.at[j])
        total = (rs2[j, 0] + rs2[j, 1]) + (rs2[j, 2] + rs2[j, 3])
        for h in range(2):
            at = j * TILES + h * PER
            flat_ss[at : at + PER, :] = total[:, h * CAP : (h + 1) * CAP]
        exchange(
            lambda q: ss.at[pl.ds(j * TILES + q, 1)], lambda q: ys.at[pl.ds(j * TILES + q, 1)], sf.at[0], sf.at[1]
        )
        ys[j * TILES + p] = ss[j * TILES + p]

    flat_s2 = s2.reshape(TILES * 16, WG)

    def product_step(j):
        value = pot[j]
        field = psi[j] * jnp.concatenate([value, value], axis=1)
        rows = dot3(split(field), pair(wave_zt))
        rows = jnp.concatenate([rows[:, :WG], rows[:, WG:]], axis=0)
        rows = dot3(pair(wave_xt), split(rows))
        for n in range(4):
            flat_s2[pl.ds(4 * j + n, TILES, stride=16), :] = rows[n * TILES : (n + 1) * TILES]

    def product_send(j):
        exchange(lambda q: s2.at[q, plane_rows[j]], lambda q: r2.at[q, plane_rows[j]], a2.at[0], a2.at[1])

    density_step(0)
    product_step(0)
    density_step(1)
    across(0)
    product_step(1)
    density_step(2)
    across(1)
    gather_bands(0)
    product_step(2)
    density_step(3)

    across(2)
    gather_bands(1)
    across(3)
    gather_bands(2)
    gather_bands(3)
    @pl.when(heavy)
    def _():
        def send(k, _):
            q = lax.rem(p + k, TILES)
            pltpu.make_async_remote_copy(
                pk.at[q, pl.ds(0, 9)], pr.at[p % SRC, pl.ds(0, 9)], pt_s, pt_r.at[p % SRC],
                device_id={"pw": q}, device_id_type=MESH,
            ).start()
            return 0

        lax.fori_loop(1, TILES, send, 0)
        pr[p % SRC, 0:9] = pk[p, 0:9]


    product_step(3)

    r2[p] = s2[p]

    drain(ys.at[pl.ds(0, SLAB * (TILES - 1))], sf.at[1])
    lines = ys.reshape(SLAB * TILES, CAP)[...]
    mean = jnp.sum(lines, axis=0, keepdims=True) * (1.0 / NG)
    modes = dot3(pair(basis_y), split(lines - mean))
    modes = modes + jnp.where(iota((NG, CAP), 0) == 0, math.sqrt(NG) * mean, 0.0)
    sb.reshape((SLAB + 1) * TILES, CAP)[...] = dot3(pair(back_y), split(modes * green[...]))
    for n, group in enumerate(GROUPS):
        exchange(lambda q: sb.at[group, q], lambda q: g.at[group, b, q], bk_s, bk_r.at[n])
        g[group, b, p] = sb[group, p]

    product_send(0)
    product_send(1)
    product_send(2)
    product_send(3)
    def point_step(i):
        @pl.when(SRC * b + i != p)
        def _():
            drain(pr.at[i, pl.ds(0, 9)], pt_r.at[i])

        data = pr[i, 0:9]
        place = data[8:9].astype(jnp.int32)
        at_x = place // (SLAB * NG)
        at_y = lax.rem(place // NG, SLAB)
        at_z = lax.rem(place, NG)
        grid = iota((NG, CAP), 0)
        on = [grid == at_x, grid == lax.rem(at_x + 1, NG)]
        for dz in range(2):
            cell = jnp.where(grid == lax.rem(at_z + dz, NG), 1.0, 0.0)
            pick[i, :, dz * CAP : (dz + 1) * CAP] = cell.astype(BF16)
            for y in range(SLAB + 1):
                value = []
                for dx in range(2):
                    first = jnp.where(at_y == y, data[4 * dx + dz : 4 * dx + dz + 1], 0.0)
                    value.append(jnp.where(at_y == y - 1, data[4 * dx + 2 + dz : 4 * dx + 3 + dz], first))
                value = jnp.where(on[0], value[0], jnp.where(on[1], value[1], 0.0))
                wst[i, y, :, dz * CAP : (dz + 1) * CAP] = value
        part[i] = jnp.zeros((8, 2 * CAP), F32)

    for i in range(SRC):
        point_step(i)

    def modes_of(y, band):
        return g.at[GROUPS[y], band]

    def pass_on(y, k):
        block = modes_of(y, lax.rem(x + chips - k, chips) * 2 + c)
        pltpu.make_async_remote_copy(
            block, block, g2_s.at[y, k], g2_r.at[y, k], device_id={"band": partner}, device_id_type=MESH
        ).start()

    def gather_start(y):
        drain(g.at[GROUPS[y], 0, others], bk_r.at[y])

        def send_x(k, _):
            to = lax.rem(x + k, chips)
            pltpu.make_async_remote_copy(
                modes_of(y, b), modes_of(y, b), g1_s.at[y, k], g1_r.at[y, k],
                device_id={"band": 2 * to + c}, device_id_type=MESH,
            ).start()
            return 0

        lax.fori_loop(1, chips, send_x, 0)
        pass_on(y, 0)

    def forward(y):
        def step(k, _):
            drain(modes_of(y, lax.rem(x + chips - k, chips) * 2 + c), g1_r.at[y, k])
            pass_on(y, k)
            return 0

        lax.fori_loop(1, chips, step, 0)

    flat_g = g.reshape((SLAB + 1) * BANDS * TILES, CAP)

    def group_step(y):
        def arrived(k, _):
            drain(modes_of(y, lax.rem(x + chips - k, chips) * 2 + 1 - c), g2_r.at[y, k])
            return 0

        lax.fori_loop(0, chips, arrived, 0)

    def plane_step(y):
        rows = flat_g[y * BANDS * TILES : (y + 1) * BANDS * TILES, :].reshape(BANDS, 2, PER, CAP)
        modes = jnp.concatenate([rows[:, h].reshape(NG, CAP) for h in range(2)], axis=1)
        plane = dot3(pair(basis_t), split(modes))
        high, low = split(dot3(split(plane), pair(basis)))

        for i in range(SRC):
            lines = dot(high, pick[i]) + dot(low, pick[i])
            lines = (lines * wst[i, y]).reshape(NG // 8, 8, 2 * CAP)
            part[i] = part[i] + jnp.sum(lines, axis=0)

    for n in range(len(GROUPS)):
        gather_start(n)
    for n in range(len(GROUPS)):
        forward(n)
    for n, group in enumerate(GROUPS):
        group_step(n)
        for y in range(group.start, group.start + group.size):
            plane_step(y)

    def fit_sum(i, _):
        lines = jnp.sum(part[i], axis=0, keepdims=True)
        o[i] = lines[:, :CAP] + lines[:, CAP:]
        return 0

    lax.fori_loop(0, SRC, fit_sum, 0)

    def fit_send(n, _):
        to, i = n // SRC, lax.rem(n, SRC)

        @pl.when(jnp.logical_not(jnp.logical_and(to == b, SRC * b + i == p)))
        def _():
            pltpu.make_async_remote_copy(
                o.at[i], f.at[p], fin.at[0], fin.at[1],
                device_id={"band": to, "pw": SRC * b + i}, device_id_type=MESH,
            ).start()
        return 0

    lax.fori_loop(0, BANDS * SRC, fit_send, 0)

    @pl.when(heavy)
    def _():
        f[p] = o[p % SRC]

    drain(r2.at[others], a2.at[1])
    flat_r2 = r2.reshape(TILES * 16, WG)
    cube = jnp.concatenate([flat_r2[pl.ds(i, 2 * NG, stride=2), :] for i in range(2)], axis=1)
    cube = dot3(pair(wave_yt), split(cube))
    for k in range(2):
        for i in range(2):
            action[0, k, i] = cube[k * WG : (k + 1) * WG, i * WG : (i + 1) * WG] * (masks[i] * SCALE_OUT)

    drain(s1.at[others], a1_s)
    drain(s2.at[others], a2.at[0])
    drain(ss.at[pl.ds(0, SLAB * (TILES - 1))], sf.at[0])
    drain(sb.at[:, others], bk_s)

    @pl.when(heavy)
    def _():
        drain(pk.at[others, pl.ds(0, 9)], pt_s)

    def sent(j, _):
        drain(rs1.at[j], t1_s.at[j])
        drain(rs1.at[j, pl.ds(0, chips - 1)], t2_s.at[j])
        return 0

    lax.fori_loop(0, SLAB, sent, 0)

    def passed(y):
        for k in range(chips):
            drain(modes_of(y, b), g2_s.at[y, k])
            if k > 0:
                drain(modes_of(y, b), g1_s.at[y, k])

    for y in range(len(GROUPS)):
        passed(y)

    @pl.when(heavy)
    def _():
        drain(f.at[others], fin.at[1])
        drain(f.at[others], fin.at[0])

    @pl.when(jnp.logical_not(heavy))
    def _():
        drain(f, fin.at[1])
        drain(f, fin.at[0])

    live = iota((TILES, CAP), 1).astype(F32) < as_column(count[...].astype(F32))
    fit[0] = jnp.where(live, f.reshape(TILES, CAP)[...], 0.0)


def body(coefficients, halfwidth, occupation, potential, corner, weight, count):
    held = {name: jnp.asarray(table) for name, table in tables().items()}
    late = [held[name] for name in LATE]
    vmem = pl.BlockSpec(memory_space=pltpu.VMEM)
    anywhere = pl.BlockSpec(memory_space=pl.ANY)
    dma = pltpu.SemaphoreType.DMA
    block = lambda *shape: pltpu.VMEM(shape, F32)
    short = lambda *shape: pltpu.VMEM(shape, BF16)
    scratch = [short(*table.shape) for table in late]
    scratch += [
        block(*coefficients.shape),
        block(SLAB, NG, NG),
        pltpu.VMEM((1, TILES, CAP), jnp.int32),
        block(8, 1, TILES, CAP),
        block(TILES, 16, WG),
        block(TILES, 16, WG),
        block(TILES, 16, WG),
        block(TILES, 16, WG),
        block(SLAB, NG, 2 * NG),
        block(SLAB, BANDS // 2, 2, PER, NG),
        block(SLAB, BANDS // 2, PER, NG),
        block(SLAB, BANDS // 2, PER, NG),
        block(SLAB * TILES, 1, CAP),
        block(SLAB * TILES, 1, CAP),
        block(SLAB + 1, TILES, 1, CAP),
        block(SLAB + 1, BANDS, TILES, 1, CAP),
        block(NG, CAP),
        block(TILES, 16, CAP),
        block(SRC, 16, CAP),
        block(SRC, SLAB + 1, NG, 2 * CAP),
        short(SRC, NG, 2 * CAP),
        block(SRC, 8, 2 * CAP),
        block(SRC, 1, CAP),
        block(TILES, 1, CAP),
    ]
    planes = (len(GROUPS), BANDS // 2)
    scratch += [
        dma((SLAB + 3 + len(late),)),
        dma(()), dma((SLAB,)), dma((2,)),
        dma(()), dma((SRC,)),
        dma((SLAB,)), dma((SLAB,)), dma((SLAB,)), dma((SLAB,)),
        dma((2,)), dma(()), dma((len(GROUPS),)),
        dma(planes), dma(planes), dma(planes), dma(planes),
        dma((2,)),
    ]
    return pl.pallas_call(
        kernel,
        out_shape=(
            jax.ShapeDtypeStruct(coefficients.shape, F32),
            jax.ShapeDtypeStruct(corner.shape, F32),
        ),
        in_specs=[vmem, pl.BlockSpec(memory_space=pltpu.SMEM), vmem, anywhere] + [anywhere] * (3 + len(late)),
        out_specs=(vmem, vmem),
        scratch_shapes=scratch,
        compiler_params=pltpu.CompilerParams(
            collective_id=0, has_side_effects=True, vmem_limit_bytes=60 * 1024 * 1024
        ),
    )(halfwidth, occupation, count, coefficients, *late[:1], potential, corner, weight, *late[1:])


def solution(mesh):
    placed = (
        P("band", None, "pw", None, None),
        P("pw", None),
        P("band"),
        P(None, "pw", None),
        P("pw", None, None),
        P(None, "pw", None, None),
        P("pw", None),
    )
    return jax.shard_map(
        body,
        mesh=mesh,
        in_specs=placed,
        out_specs=(P("band", None, "pw", None, None), P("pw", None, None)),
        check_vma=False,
    )
```

time: 121 us -> 109 us (0.901)
  Pallas kernels: 112 us -> 105 us
  local copies, waits for them, and re-layouts: 6.83 us -> 2.29 us
    pallas_call x1, Pallas kernels: 112 us -> 105 us  [body(): pl.pallas_call(kernel, out_shape=(jax.ShapeDtypeStruct(coefficients.shape...]
    unnamed x18 -> x4, local copies, waits for them, and re-layouts: 6.83 us -> 2.29 us
where the time goes in v3:
time: 109 us
  Pallas kernels  105 us (96%)
  local copies, waits for them, and re-layouts  2.29 us (2%)
  between operations  1.29 us (1%)
    pallas_call x1, Pallas kernels, body(): pl.pallas_call(kernel, out_shape=(jax.ShapeDtypeStruct(coefficients.shape...  105 us
    unnamed x4, local copies, waits for them, and re-layouts  2.29 us

profile of v3, /device:TPU:1, one launch (start us, length us, event | category | flops | bytes accessed | tf_op | source)
XLA Modules:
  0.0 108.8 jit_solution(196564077882644254)
XLA Ops:
  1.3 105.2 %shard_map.176 = (f32[1,2,2,128,128]{4,3,2,1,0:T(8,128)}, f32[1,64,128]{2,1,0:T(8,128)}) custom-call(s32[2,128]{1,0:T(2,128)} %half.1, f32[1]{0:T(128)S(6)} %copy.21.occupation, s32[1,64]{1,0:T(1,128)} %count.1, f32[1,2,2,128,128]{4,3,2,1,0:T(8,128)} %coef_h.1, bf16[2,512,256]{2,1,0:T(8,128)(2,1)} %constant.20.clone.wave_y_h, f32[256,4,256]{2,1,0:T(4,128)} %potential.1, ...), custom_call_target="tpu_custom_call" | custom-call | tf_op jit(solution)/shard_map/pallas_call | solution.py:527
  106.5 0.0 copy-start
  106.5 1.7 %copy.22 = f32[1,2,2,128,128]{4,3,2,1,0:T(8,128)} copy(f32[1,2,2,128,128]{4,3,2,1,0:T(8,128)} %get-tuple-element.4) | data formatting | bytes 524288
  108.2 0.0 copy-done
  108.2 0.6 copy.23
Async XLA Ops:
  106.5 1.7 %copy-start = (f32[1,64,128]{2,1,0:T(8,128)S(1)}, f32[1,64,128]{2,1,0:T(8,128)}, u32[]{:S(2)}) copy-start(f32[1,64,128]{2,1,0:T(8,128)} %get-tuple-element.5) | copy-start | bytes 98308

commit v4 on v3

--- a/solution.py
+++ b/solution.py
@@ -103,8 +103,8 @@
     action, fit,
     wave_y, wave_x, wave_z, basis_t, basis, wave_zt, wave_xt, basis_y, back_y, wave_yt,
     coef, pot, corn, weig,
-    s1, r1, s2, r2, psi, sr, rs1, rs2, ss, ys, sb, g, green, pk, pr, wst, pick, part, o, f,
-    load_sem, a1_s, a1_r, a2, pt_s, pt_r, t1_s, t1_r, t2_s, t2_r, sf, bk_s, bk_r, g1_s, g1_r, g2_s, g2_r, fin,
+    s1, r1, s2, r2, psi, sr, rs1, rs2, ss, ys, sb, g, green, pk, pr, wst, pick, part, o, f, f2,
+    load_sem, a1_s, a1_r, a2, pt_s, pt_r, t1_s, t1_r, t2_s, t2_r, sf, bk_s, bk_r, g1_s, g1_r, g2_s, g2_r, fin, fan,
 ):
     b = lax.axis_index("band")
     p = lax.axis_index("pw")
@@ -133,14 +133,6 @@
         return 0
 
     lax.fori_loop(1, TILES, greet_pw, 0)
-
-    def greet_fit(q, _):
-        @pl.when(jnp.logical_not(jnp.logical_and(heavy, q == p)))
-        def _():
-            pl.semaphore_signal(barrier, inc=1, device_id={"band": p // SRC, "pw": q}, device_id_type=MESH)
-        return 0
-
-    lax.fori_loop(0, TILES, greet_fit, 0)
 
     def greet_band(k, _):
         pl.semaphore_signal(barrier, inc=1, device_id={"band": lax.rem(b + k, BANDS)}, device_id_type=MESH)
@@ -167,13 +159,7 @@
         flat_s1[pl.ds(i, 2 * NG, stride=2), :] = section[:, i * WG : (i + 1) * WG]
     r1[p] = s1[p]
 
-    @pl.when(heavy)
-    def _():
-        pl.semaphore_wait(barrier, TILES - 1 + BANDS - 1 + TILES - 1)
-
-    @pl.when(jnp.logical_not(heavy))
-    def _():
-        pl.semaphore_wait(barrier, TILES - 1 + BANDS - 1 + TILES)
+    pl.semaphore_wait(barrier, TILES - 1 + BANDS - 1)
 
     def exchange(source, target, send_sem, recv_sem):
         def send(k, _):
@@ -415,22 +401,15 @@
 
     lax.fori_loop(0, SRC, fit_sum, 0)
 
-    def fit_send(n, _):
-        to, i = n // SRC, lax.rem(n, SRC)
-
-        @pl.when(jnp.logical_not(jnp.logical_and(to == b, SRC * b + i == p)))
+    def fit_send(i, _):
+        @pl.when(SRC * b + i != p)
         def _():
             pltpu.make_async_remote_copy(
-                o.at[i], f.at[p], fin.at[0], fin.at[1],
-                device_id={"band": to, "pw": SRC * b + i}, device_id_type=MESH,
+                o.at[i], f.at[p], fin.at[0], fin.at[1], device_id={"pw": SRC * b + i}, device_id_type=MESH
             ).start()
         return 0
 
-    lax.fori_loop(0, BANDS * SRC, fit_send, 0)
-
-    @pl.when(heavy)
-    def _():
-        f[p] = o[p % SRC]
+    lax.fori_loop(0, SRC, fit_send, 0)
 
     drain(r2.at[others], a2.at[1])
     flat_r2 = r2.reshape(TILES * 16, WG)
@@ -440,6 +419,20 @@
         for i in range(2):
             action[0, k, i] = cube[k * WG : (k + 1) * WG, i * WG : (i + 1) * WG] * (masks[i] * SCALE_OUT)
 
+    @pl.when(heavy)
+    def _():
+        f[p] = o[p % SRC]
+        drain(f.at[others], fin.at[1])
+
+        def spread(k, _):
+            pltpu.make_async_remote_copy(
+                f, f2, fan.at[0], fan.at[1], device_id={"band": lax.rem(b + k, BANDS)}, device_id_type=MESH
+            ).start()
+            return 0
+
+        lax.fori_loop(1, BANDS, spread, 0)
+        f2[...] = f[...]
+
     drain(s1.at[others], a1_s)
     drain(s2.at[others], a2.at[0])
     drain(ss.at[pl.ds(0, SLAB * (TILES - 1))], sf.at[0])
@@ -467,16 +460,16 @@
 
     @pl.when(heavy)
     def _():
-        drain(f.at[others], fin.at[1])
-        drain(f.at[others], fin.at[0])
+        drain(o.at[pl.ds(0, SRC - 1)], fin.at[0])
+        drain(g.at[0, pl.ds(0, BANDS - 1)], fan.at[0])
 
     @pl.when(jnp.logical_not(heavy))
     def _():
-        drain(f, fin.at[1])
-        drain(f, fin.at[0])
+        drain(o, fin.at[0])
+        drain(f2, fan.at[1])
 
     live = iota((TILES, CAP), 1).astype(F32) < as_column(count[...].astype(F32))
-    fit[0] = jnp.where(live, f.reshape(TILES, CAP)[...], 0.0)
+    fit[0] = jnp.where(live, f2.reshape(TILES, CAP)[...], 0.0)
 
 
 def body(coefficients, halfwidth, occupation, potential, corner, weight, count):
@@ -513,6 +506,7 @@
         block(SRC, 8, 2 * CAP),
         block(SRC, 1, CAP),
         block(TILES, 1, CAP),
+        block(TILES, 1, CAP),
     ]
     planes = (len(GROUPS), BANDS // 2)
     scratch += [
@@ -522,7 +516,7 @@
         dma((SLAB,)), dma((SLAB,)), dma((SLAB,)), dma((SLAB,)),
         dma((2,)), dma(()), dma((len(GROUPS),)),
         dma(planes), dma(planes), dma(planes), dma(planes),
-        dma((2,)),
+        dma((2,)), dma((2,)),
     ]
     return pl.pallas_call(
         kernel,

time: 109 us -> 108 us (level); the launches traced: 109 us -> 106 us
  Pallas kernels: 105 us -> 103 us
    pallas_call x1, Pallas kernels: 105 us -> 103 us  [body(): pl.pallas_call(kernel, out_shape=(jax.ShapeDtypeStruct(coefficients.shape...]
where the time goes in v4:
time: 108 us; the launch traced here: 106 us
  Pallas kernels  103 us (95%)
  local copies, waits for them, and re-layouts  2.29 us (2%)
  between operations  1.29 us (1%)
    pallas_call x1, Pallas kernels, body(): pl.pallas_call(kernel, out_shape=(jax.ShapeDtypeStruct(coefficients.shape...  103 us
    unnamed x4, local copies, waits for them, and re-layouts  2.29 us

profile of v4, /device:TPU:1, one launch (start us, length us, event | category | flops | bytes accessed | tf_op | source)
XLA Modules:
  0.0 106.4 jit_solution(12815522408597691537)
XLA Ops:
  1.3 102.9 %shard_map.176 = (f32[1,2,2,128,128]{4,3,2,1,0:T(8,128)}, f32[1,64,128]{2,1,0:T(8,128)}) custom-call(s32[2,128]{1,0:T(2,128)} %half.1, f32[1]{0:T(128)S(6)} %copy.21.occupation, s32[1,64]{1,0:T(1,128)} %count.1, f32[1,2,2,128,128]{4,3,2,1,0:T(8,128)} %coef_h.1, bf16[2,512,256]{2,1,0:T(8,128)(2,1)} %constant.20.clone.wave_y_h, f32[256,4,256]{2,1,0:T(4,128)} %potential.1, ...), custom_call_target="tpu_custom_call" | custom-call | tf_op jit(solution)/shard_map/pallas_call | solution.py:521
  104.1 0.0 copy-start
  104.2 1.7 %copy.22 = f32[1,2,2,128,128]{4,3,2,1,0:T(8,128)} copy(f32[1,2,2,128,128]{4,3,2,1,0:T(8,128)} %get-tuple-element.4) | data formatting | bytes 524288
  105.8 0.0 copy-done
  105.8 0.6 copy.23
Async XLA Ops:
  104.1 1.7 %copy-start = (f32[1,64,128]{2,1,0:T(8,128)S(1)}, f32[1,64,128]{2,1,0:T(8,128)}, u32[]{:S(2)}) copy-start(f32[1,64,128]{2,1,0:T(8,128)} %get-tuple-element.5) | copy-start | bytes 98308
